TPU v7x, 512 devices: a whole 4x8x8 slice. The times are simulated.
512 devices in a mesh: gx: 32 (over y, x), gy: 16 (over z, core).
Axes of the slice: x: 4, y: 8, z: 8, core: 2. Of those that a mesh axis runs over, the one named last changes fastest.
Arguments:
- probes: bfloat16 [16, 2, 12, 256, 4096], P(None, None, None, 'gx', 'gy'), may hold values from -120 to 120
- material: int32 [12, 256, 4096], P(None, 'gx', 'gy'), may hold values from 0 to 3
- visc_table: float32 [4], replicated, may hold values from 0.5 to 2
- brink_table: float32 [4], replicated, may hold values from 0.1 to 10
- cond_table: float32 [4], replicated, may hold values from 0.5 to 2
- base_flow: float32 [12, 256, 4096], P(None, 'gx', 'gy'), may hold values from 0 to 1
Outputs:
- basis: float32 [16, 2, 12, 256, 4096], P(None, None, None, 'gx', 'gy')
- r_factor: float32 [16, 16], replicated
All inputs are finite; a program needn't handle non-finite values.
Results may differ from a plain program's by a relative error of at most 0.0003.
Values may be sent and summed in bfloat16 or wider, within the bound.
No kernel may reach another device: no remote copies, remote signals or barrier semaphores. Data moves between devices by JAX's collectives and lax.ppermute only.
A program may use at most 64 MiB of HBM per device.

v0:
```python
import math

import jax
import jax.numpy as jnp
from jax import lax
from jax.sharding import PartitionSpec as P


def with_halo(block, sides, width):
    for axis, dim in sides:
        count = lax.axis_size(axis)
        forward = [(i, i + 1) for i in range(count - 1)]
        backward = [(target, source) for source, target in forward]
        low = lax.ppermute(
            lax.slice_in_dim(block, block.shape[dim] - width, None, axis=dim), axis, forward
        )
        high = lax.ppermute(lax.slice_in_dim(block, 0, width, axis=dim), axis, backward)
        block = jnp.concatenate([low, block, high], axis=dim)
    return block


def from_partner(array, axis, bit):
    return lax.ppermute(array, axis, [(i, i ^ 1 << bit) for i in range(lax.axis_size(axis))])


def cell_values(material, table):
    total = jnp.zeros(material.shape, jnp.float32)
    for index in range(table.shape[0]):
        total = total + jnp.where(material == index, table[index], jnp.float32(0.0))
    return total


def lap_parts(field):
    center = field[:, :, 1:-1, 1:-1]
    vertical = jnp.pad(center, ((0, 0), (1, 1), (0, 0), (0, 0)))
    beside = (
        field[:, :, 2:, 1:-1]
        + field[:, :, :-2, 1:-1]
        + field[:, :, 1:-1, 2:]
        + field[:, :, 1:-1, :-2]
    )
    beside = beside + vertical[:, 2:] + vertical[:, :-2]
    return (center, 6.0 * center - beside, vertical[:, :-2])


def apply_operator(padded, material, visc_table, brink_table, cond_table, base_flow):
    wide = padded.astype(jnp.float32)
    w_center, w_lap, w_below = lap_parts(wide[:, 0])
    t_center, t_lap, t_below = lap_parts(wide[:, 1])
    visc = cell_values(material, visc_table)
    brink = cell_values(material, brink_table)
    cond = cell_values(material, cond_table)
    image_w = visc * w_lap + brink * w_center - t_center
    image_t = cond * t_lap + 0.5 * w_center + base_flow * (t_center - t_below)
    return jnp.stack([image_w, image_t], axis=1)


def merge_factors(upper_own, upper_other):
    gram = jnp.dot(upper_own.T, upper_own, precision=lax.Precision.HIGHEST)
    gram = gram + jnp.dot(upper_other.T, upper_other, precision=lax.Precision.HIGHEST)
    return jnp.linalg.cholesky(gram).T


def on_device(probes, material, visc_table, brink_table, cond_table, base_flow):
    padded = with_halo(probes, (("gx", 3), ("gy", 4)), 1)
    image = apply_operator(padded, material, visc_table, brink_table, cond_table, base_flow)
    flat = image.reshape(image.shape[0], -1)
    local_gram = jnp.dot(flat, flat.T, precision=lax.Precision.HIGHEST)
    upper = jnp.linalg.cholesky(local_gram).T
    for bit_x in range(lax.axis_size("gx").bit_length() - 1):
        partner = from_partner(upper, "gx", bit_x)
        upper = merge_factors(upper, partner)
    for bit_y in range(lax.axis_size("gy").bit_length() - 1):
        partner = from_partner(upper, "gy", bit_y)
        upper = merge_factors(upper, partner)
    rows_total = flat.shape[1] * lax.axis_size("gx") * lax.axis_size("gy")
    scale = math.sqrt(rows_total)
    solved = jax.scipy.linalg.solve_triangular(upper.T, flat, lower=True)
    basis = (solved * scale).reshape(image.shape)
    return (basis, upper / scale)


def solution(mesh):
    in_specs = (
        P(None, None, None, "gx", "gy"),
        P(None, "gx", "gy"),
        P(),
        P(),
        P(),
        P(None, "gx", "gy"),
    )
    out_specs = (P(None, None, None, "gx", "gy"), P())
    return jax.shard_map(
        on_device, mesh=mesh, in_specs=in_specs, out_specs=out_specs, check_vma=False
    )
```

profile of v0, /device:TPU:30, one launch (start us, length us, event | category | flops | bytes accessed | tf_op | source)
XLA Modules:
  0.0 152.6 jit_solution(616662088091494591)
XLA Ops:
  0.7 2.7 %fusion.107 = (bf16[16,2,12,1,256]{4,3,2,1,0:T(2,128)(2,1)S(1)}, bf16[16,2,12,1,256]{4,3,2,1,0:T(2,128)(2,1)S(1)}) fusion(bf16[16,2,12,8,256]{4,3,2,1,0:T(8,128)(2,1)} %param.7), kind=kLoop, calls=%fused_computation.177 | loop fusion | bytes 786432 | tf_op jit(solution)/shard_map/slice | solution.py:17
  3.5 4.6 %collective-permute-start = (bf16[16,2,12,1,256]{4,0,3,2,1:T(8,128)(2,1)S(1)}, bf16[16,2,12,1,256]{4,0,3,2,1:T(8,128)(2,1)S(1)}, u32[]{:S(2)}, u32[]{:S(2)}) collective-permute-start(bf16[16,2,12,1,256]{4,0,3,2,1:T(8,128)(2,1)S(1)} %copy.133), channel_id=1, source_target_pairs={{0,16},{16,32},{32,48},{48,64},{64,80},{80,96},{96,112},{112,128},... | collective-permute-start | bytes 589832 | tf_op jit(solution)/shard_map/ppermute | solution.py:14
  12.1 2.6 %select_add_fusion.2 = (f32[12,8,256]{2,1,0:T(8,128)S(1)}, pred[12,8,256]{2,1,0:T(8,128)(4,1)S(1)}, pred[12,8,256]{2,1,0:T(8,128)(4,1)S(1)}, pred[12,8,256]{2,1,0:T(8,128)(4,1)S(1)}, pred[12,8,256]{2,1,0:T(8,128)(4,1)S(1)}) fusion(f32[]{:T(128)} %bitcast.3, f32[]{:T(128)} %bitcast.2, f32[]{:T(128)} %bitcast.1, f32[]{:T(128)} %bitcast, ...), kind=kLoop, calls=%fused_computation.41 | loop fusion | flops 270336 | bytes 294928 | tf_op jit(solution)/shard_map/add | solution.py:29
  15.6 4.1 %collective-permute-done.1 = bf16[16,2,12,1,256]{4,0,3,2,1:T(8,128)(2,1)S(1)} collective-permute-done((bf16[16,2,12,1,256]{4,0,3,2,1:T(8,128)(2,1)S(1)}, bf16[16,2,12,1,256]{4,0,3,2,1:T(8,128)(2,1)S(1)}, u32[]{:S(2)}, u32[]{:S(2)}) %collective-permute-start.1) | collective-permute-done | bytes 196640 | tf_op jit(solution)/shard_map/ppermute | solution.py:17
  21.2 3.3 %copy.76 = bf16[16,2,12,10,1]{0,1,4,3,2:T(2,128)(2,1)} copy(bf16[16,2,12,10,1]{4,0,3,2,1:T(8,128)(2,1)} %get-tuple-element.18) | data formatting | bytes 15360 | tf_op jit(solution)/shard_map/slice | solution.py:15
  27.3 3.7 %collective-permute-start.2 = (bf16[16,2,12,10,1]{0,1,4,3,2:T(2,128)(2,1)}, bf16[16,2,12,10,1]{0,1,4,3,2:T(2,128)(2,1)}, u32[]{:S(2)}, u32[]{:S(2)}) collective-permute-start(bf16[16,2,12,10,1]{0,1,4,3,2:T(2,128)(2,1)} %copy.76), channel_id=1, source_target_pairs={{0,1},{1,2},{2,3},{3,4},{4,5},{5,6},{6,7},{7,8},{8,9},{9,10},{10,1... | collective-permute-start | bytes 23048 | tf_op jit(solution)/shard_map/ppermute | solution.py:14
  30.9 5.0 %select_add_fusion.1 = (f32[12,8,256]{2,1,0:T(8,128)S(1)}, f32[12,8,256]{2,1,0:T(8,128)S(1)}) fusion(pred[12,8,256]{2,1,0:T(8,128)(4,1)S(1)} %get-tuple-element.13, pred[12,8,256]{2,1,0:T(8,128)(4,1)S(1)} %get-tuple-element.12, pred[12,8,256]{2,1,0:T(8,128)(4,1)S(1)} %get-tuple-element.11, pred[12,8,256]{2,1,0:T(8,128)(4,1)S(1)} %get-tuple-element.10, ...), kind=kLoop, calls=%fused_computation.40 | loop fusion | flops 344064 | bytes 294944 | tf_op jit(solution)/shard_map/add | solution.py:29
  36.0 2.3 %copy.78 = bf16[16,2,12,10,1]{4,0,3,2,1:T(8,128)(2,1)S(1)} copy(bf16[16,2,12,10,1]{0,1,4,3,2:T(2,128)(2,1)} %collective-permute-done.2) | data formatting | bytes 15360 | tf_op jit(solution)/shard_map/ppermute | solution.py:14
  38.3 2.4 %copy.79 = bf16[16,2,12,10,1]{4,0,3,2,1:T(8,128)(2,1)} copy(bf16[16,2,12,10,1]{0,1,4,3,2:T(2,128)(2,1)S(1)} %collective-permute-done.3) | data formatting | bytes 15360 | tf_op jit(solution)/shard_map/ppermute | solution.py:17
  40.7 2.7 %maximum_convert_fusion = f32[16,2,12,10,258]{4,0,3,2,1:T(8,128)S(1)} fusion(bf16[16,2,12,10,1]{4,0,3,2,1:T(8,128)(2,1)} %copy.79, bf16[16,2,12,10,256]{4,0,3,2,1:T(8,128)(2,1)S(1)} %constant_dynamic-update-slice_fusion, bf16[16,2,12,10,1]{4,0,3,2,1:T(8,128)(2,1)S(1)} %copy.78), kind=kLoop, calls=%fused_computation.4 | loop fusion | flops 5944320 | bytes 5944320 | tf_op jit(solution)/shard_map/convert_element_type | solution.py:47
  45.2 3.8 %fusion.6 = (f32[16,1,12,8,256]{4,0,3,2,1:T(8,128)S(1)}, f32[16,1,12,8,256]{4,0,3,2,1:T(8,128)S(1)}) fusion(f32[16,12,8,256]{3,0,2,1:T(8,128)S(1)} %slice.144, f32[16,12,10,258]{3,0,2,1:T(8,128)S(1)} %get-tuple-element.16, f32[12,8,256]{2,1,0:T(8,128)S(1)} %get-tuple-element.22, f32[12,8,256]{2,1,0:T(8,128)S(1)} %get-tuple-element.9, ...), kind=kLoop, calls=%fused_computation.15 | loop fusion | flops 9437184 | bytes 22413312 | tf_op jit(solution)/shard_map/stack | solution.py:55
  49.0 4.0 %convolution_bitcast_fusion = f32[16,16]{1,0:T(8,128)S(1)} fusion(f32[16,1,12,8,256]{4,0,3,2,1:T(8,128)S(1)} %get-tuple-element.15, f32[16,1,12,8,256]{4,0,3,2,1:T(8,128)S(1)} %get-tuple-element.14), kind=kOutput, calls=%fused_computation.38 | convolution fusion | flops 151781376 | bytes 3146752 | tf_op jit(solution)/shard_map/dot_general | solution.py:68
  59.2 3.0 %collective-permute-done.4 = f32[16,16]{0,1:T(8,128)S(1)} collective-permute-done((f32[16,16]{0,1:T(8,128)S(1)}, f32[16,16]{0,1:T(8,128)S(1)}, u32[]{:S(2)}, u32[]{:S(2)}) %collective-permute-start.4) | collective-permute-done | bytes 1056 | tf_op jit(solution)/shard_map/ppermute | solution.py:23
  67.9 4.3 %collective-permute-done.5 = f32[16,16]{0,1:T(8,128)S(1)} collective-permute-done((f32[16,16]{0,1:T(8,128)S(1)}, f32[16,16]{0,1:T(8,128)S(1)}, u32[]{:S(2)}, u32[]{:S(2)}) %collective-permute-start.5) | collective-permute-done | bytes 1056 | tf_op jit(solution)/shard_map/ppermute | solution.py:23
  78.0 2.8 %collective-permute-done.6 = f32[16,16]{0,1:T(8,128)S(1)} collective-permute-done((f32[16,16]{0,1:T(8,128)S(1)}, f32[16,16]{0,1:T(8,128)S(1)}, u32[]{:S(2)}, u32[]{:S(2)}) %collective-permute-start.6) | collective-permute-done | bytes 1056 | tf_op jit(solution)/shard_map/ppermute | solution.py:23
  83.8 1.9 %collective-permute-start.7 = (f32[16,16]{0,1:T(8,128)S(1)}, f32[16,16]{0,1:T(8,128)S(1)}, u32[]{:S(2)}, u32[]{:S(2)}) collective-permute-start(f32[16,16]{0,1:T(8,128)S(1)} %fusion.49), channel_id=1, source_target_pairs={{0,128},{16,144},{32,160},{48,176},{64,192},{80,208},{96,224},{112... | collective-permute-start | bytes 3080 | tf_op jit(solution)/shard_map/ppermute | solution.py:23
  86.5 3.7 %collective-permute-done.7 = f32[16,16]{0,1:T(8,128)S(1)} collective-permute-done((f32[16,16]{0,1:T(8,128)S(1)}, f32[16,16]{0,1:T(8,128)S(1)}, u32[]{:S(2)}, u32[]{:S(2)}) %collective-permute-start.7) | collective-permute-done | bytes 1056 | tf_op jit(solution)/shard_map/ppermute | solution.py:23
  93.3 1.9 %collective-permute-start.8 = (f32[16,16]{0,1:T(8,128)S(1)}, f32[16,16]{0,1:T(8,128)S(1)}, u32[]{:S(2)}, u32[]{:S(2)}) collective-permute-start(f32[16,16]{0,1:T(8,128)S(1)} %fusion.51), channel_id=1, source_target_pairs={{0,256},{16,272},{32,288},{48,304},{64,320},{80,336},{96,352},{112... | collective-permute-start | bytes 3080 | tf_op jit(solution)/shard_map/ppermute | solution.py:23
  96.0 6.7 %collective-permute-done.8 = f32[16,16]{0,1:T(8,128)S(1)} collective-permute-done((f32[16,16]{0,1:T(8,128)S(1)}, f32[16,16]{0,1:T(8,128)S(1)}, u32[]{:S(2)}, u32[]{:S(2)}) %collective-permute-start.8) | collective-permute-done | bytes 1056 | tf_op jit(solution)/shard_map/ppermute | solution.py:23
  111.8 4.0 %collective-permute-start.10 = (f32[16,16]{0,1:T(8,128)S(1)}, f32[16,16]{0,1:T(8,128)S(1)}, u32[]{:S(2)}, u32[]{:S(2)}) collective-permute-start(f32[16,16]{0,1:T(8,128)S(1)} %fusion.55), channel_id=1, source_target_pairs={{0,2},{1,3},{2,0},{3,1},{4,6},{5,7},{6,4},{7,5},{8,10},{9,11},{10,... | collective-permute-start | bytes 3080 | tf_op jit(solution)/shard_map/ppermute | solution.py:23
  120.5 6.5 %collective-permute-start.11 = (f32[16,16]{0,1:T(8,128)S(1)}, f32[16,16]{0,1:T(8,128)S(1)}, u32[]{:S(2)}, u32[]{:S(2)}) collective-permute-start(f32[16,16]{0,1:T(8,128)S(1)} %fusion.57), channel_id=1, source_target_pairs={{0,4},{1,5},{2,6},{3,7},{4,0},{5,1},{6,2},{7,3},{8,12},{9,13},{10,... | collective-permute-start | bytes 3080 | tf_op jit(solution)/shard_map/ppermute | solution.py:23
  131.4 9.1 %collective-permute-start.12 = (f32[16,16]{0,1:T(8,128)S(1)}, f32[16,16]{0,1:T(8,128)S(1)}, u32[]{:S(2)}, u32[]{:S(2)}) collective-permute-start(f32[16,16]{0,1:T(8,128)S(1)} %fusion.59), channel_id=1, source_target_pairs={{0,8},{1,9},{2,10},{3,11},{4,12},{5,13},{6,14},{7,15},{8,0},{9,1},... | collective-permute-start | bytes 3080 | tf_op jit(solution)/shard_map/ppermute | solution.py:23
  147.0 3.0 %convolution_multiply_fusion = f32[16,49152]{1,0:T(8,128)S(1)} fusion(f32[16,49152]{1,0:T(8,128)S(1)} %bitcast.115, f32[1,16,16]{1,2,0:T(8,128)S(1)} %custom-call.6), kind=kOutput, calls=%fused_computation | convolution fusion | flops 151781376 | bytes 6292480 | tf_op jit(solution)/shard_map/jit(_solve_triangular)/triangular_solve | solution.py:78
  150.0 2.6 %copy.130 = f32[2,8,192,256]{3,2,1,0:T(8,128)} copy(f32[2,8,192,256]{3,1,2,0:T(8,128)S(1)} %bitcast.117) | data formatting | bytes 6291456
  (120 shorter events, 60.7 us)
Async XLA Ops:
  0.6 14.1 %copy-start = (bf16[16,2,12,8,256]{4,3,2,1,0:T(8,128)(2,1)S(1)}, bf16[16,2,12,8,256]{4,3,2,1,0:T(8,128)(2,1)}, u32[]{:S(2)}) copy-start(bf16[16,2,12,8,256]{4,3,2,1,0:T(8,128)(2,1)} %param.7) | copy-start | bytes 4718596
  0.6 9.5 %copy-start.3 = (f32[4]{0:T(128)S(1)}, f32[4]{0:T(128)}, u32[]{:S(2)}) copy-start(f32[4]{0:T(128)} %param.9) | copy-start | bytes 52
  0.7 10.2 %copy-start.4 = (f32[4]{0:T(128)S(1)}, f32[4]{0:T(128)}, u32[]{:S(2)}) copy-start(f32[4]{0:T(128)} %param.10) | copy-start | bytes 52
  0.7 10.8 %copy-start.5 = (f32[4]{0:T(128)S(1)}, f32[4]{0:T(128)}, u32[]{:S(2)}) copy-start(f32[4]{0:T(128)} %param.11) | copy-start | bytes 52
  0.7 11.4 %copy-start.2 = (s32[12,8,256]{2,1,0:T(8,128)S(1)}, s32[12,8,256]{2,1,0:T(8,128)}, u32[]{:S(2)}) copy-start(s32[12,8,256]{2,1,0:T(8,128)} %param.8) | copy-start | bytes 294916
  3.5 11.3 %collective-permute-start = (bf16[16,2,12,1,256]{4,0,3,2,1:T(8,128)(2,1)S(1)}, bf16[16,2,12,1,256]{4,0,3,2,1:T(8,128)(2,1)S(1)}, u32[]{:S(2)}, u32[]{:S(2)}) collective-permute-start(bf16[16,2,12,1,256]{4,0,3,2,1:T(8,128)(2,1)S(1)} %copy.133), channel_id=1, source_target_pairs={{0,16},{16,32},{32,48},{48,64},{64,80},{80,96},{96,112},{112,128},... | collective-permute-start | bytes 589832 | tf_op jit(solution)/shard_map/ppermute | solution.py:14
  8.2 11.6 %collective-permute-start.1 = (bf16[16,2,12,1,256]{4,0,3,2,1:T(8,128)(2,1)S(1)}, bf16[16,2,12,1,256]{4,0,3,2,1:T(8,128)(2,1)S(1)}, u32[]{:S(2)}, u32[]{:S(2)}) collective-permute-start(bf16[16,2,12,1,256]{4,0,3,2,1:T(8,128)(2,1)S(1)} %copy.134), channel_id=1, source_target_pairs={{16,0},{32,16},{48,32},{64,48},{80,64},{96,80},{112,96},{128,112},... | collective-permute-start | bytes 589832 | tf_op jit(solution)/shard_map/ppermute | solution.py:17
  26.0 12.3 %collective-permute-start.3 = (bf16[16,2,12,10,1]{0,1,4,3,2:T(2,128)(2,1)S(1)}, bf16[16,2,12,10,1]{0,1,4,3,2:T(2,128)(2,1)S(1)}, u32[]{:S(2)}, u32[]{:S(2)}) collective-permute-start(bf16[16,2,12,10,1]{0,1,4,3,2:T(2,128)(2,1)S(1)} %copy.77), channel_id=1, source_target_pairs={{1,0},{2,1},{3,2},{4,3},{5,4},{6,5},{7,6},{8,7},{9,8},{10,9},{11,1... | collective-permute-start | bytes 23048 | tf_op jit(solution)/shard_map/ppermute | solution.py:17
  27.3 8.7 %collective-permute-start.2 = (bf16[16,2,12,10,1]{0,1,4,3,2:T(2,128)(2,1)}, bf16[16,2,12,10,1]{0,1,4,3,2:T(2,128)(2,1)}, u32[]{:S(2)}, u32[]{:S(2)}) collective-permute-start(bf16[16,2,12,10,1]{0,1,4,3,2:T(2,128)(2,1)} %copy.76), channel_id=1, source_target_pairs={{0,1},{1,2},{2,3},{3,4},{4,5},{5,6},{6,7},{7,8},{8,9},{9,10},{10,1... | collective-permute-start | bytes 23048 | tf_op jit(solution)/shard_map/ppermute | solution.py:14
  44.3 0.9 copy-start.1
  56.7 5.5 %collective-permute-start.4 = (f32[16,16]{0,1:T(8,128)S(1)}, f32[16,16]{0,1:T(8,128)S(1)}, u32[]{:S(2)}, u32[]{:S(2)}) collective-permute-start(f32[16,16]{0,1:T(8,128)S(1)} %fusion.43), channel_id=1, source_target_pairs={{0,16},{16,0},{32,48},{48,32},{64,80},{80,64},{96,112},{112,96},{1... | collective-permute-start | bytes 3080 | tf_op jit(solution)/shard_map/ppermute | solution.py:23
  65.2 7.0 %collective-permute-start.5 = (f32[16,16]{0,1:T(8,128)S(1)}, f32[16,16]{0,1:T(8,128)S(1)}, u32[]{:S(2)}, u32[]{:S(2)}) collective-permute-start(f32[16,16]{0,1:T(8,128)S(1)} %fusion.45), channel_id=1, source_target_pairs={{0,32},{16,48},{32,0},{48,16},{64,96},{80,112},{96,64},{112,80},{1... | collective-permute-start | bytes 3080 | tf_op jit(solution)/shard_map/ppermute | solution.py:23
  75.3 5.5 %collective-permute-start.6 = (f32[16,16]{0,1:T(8,128)S(1)}, f32[16,16]{0,1:T(8,128)S(1)}, u32[]{:S(2)}, u32[]{:S(2)}) collective-permute-start(f32[16,16]{0,1:T(8,128)S(1)} %fusion.47), channel_id=1, source_target_pairs={{0,64},{16,80},{32,96},{48,112},{64,0},{80,16},{96,32},{112,48},{1... | collective-permute-start | bytes 3080 | tf_op jit(solution)/shard_map/ppermute | solution.py:23
  83.8 6.4 %collective-permute-start.7 = (f32[16,16]{0,1:T(8,128)S(1)}, f32[16,16]{0,1:T(8,128)S(1)}, u32[]{:S(2)}, u32[]{:S(2)}) collective-permute-start(f32[16,16]{0,1:T(8,128)S(1)} %fusion.49), channel_id=1, source_target_pairs={{0,128},{16,144},{32,160},{48,176},{64,192},{80,208},{96,224},{112... | collective-permute-start | bytes 3080 | tf_op jit(solution)/shard_map/ppermute | solution.py:23
  93.3 9.5 %collective-permute-start.8 = (f32[16,16]{0,1:T(8,128)S(1)}, f32[16,16]{0,1:T(8,128)S(1)}, u32[]{:S(2)}, u32[]{:S(2)}) collective-permute-start(f32[16,16]{0,1:T(8,128)S(1)} %fusion.51), channel_id=1, source_target_pairs={{0,256},{16,272},{32,288},{48,304},{64,320},{80,336},{96,352},{112... | collective-permute-start | bytes 3080 | tf_op jit(solution)/shard_map/ppermute | solution.py:23
  105.8 3.1 %collective-permute-start.9 = (f32[16,16]{0,1:T(8,128)S(1)}, f32[16,16]{0,1:T(8,128)S(1)}, u32[]{:S(2)}, u32[]{:S(2)}) collective-permute-start(f32[16,16]{0,1:T(8,128)S(1)} %fusion.53), channel_id=1, source_target_pairs={{0,1},{1,0},{2,3},{3,2},{4,5},{5,4},{6,7},{7,6},{8,9},{9,8},{10,11... | collective-permute-start | bytes 3080 | tf_op jit(solution)/shard_map/ppermute | solution.py:23
  111.8 5.7 %collective-permute-start.10 = (f32[16,16]{0,1:T(8,128)S(1)}, f32[16,16]{0,1:T(8,128)S(1)}, u32[]{:S(2)}, u32[]{:S(2)}) collective-permute-start(f32[16,16]{0,1:T(8,128)S(1)} %fusion.55), channel_id=1, source_target_pairs={{0,2},{1,3},{2,0},{3,1},{4,6},{5,7},{6,4},{7,5},{8,10},{9,11},{10,... | collective-permute-start | bytes 3080 | tf_op jit(solution)/shard_map/ppermute | solution.py:23
  120.5 7.9 %collective-permute-start.11 = (f32[16,16]{0,1:T(8,128)S(1)}, f32[16,16]{0,1:T(8,128)S(1)}, u32[]{:S(2)}, u32[]{:S(2)}) collective-permute-start(f32[16,16]{0,1:T(8,128)S(1)} %fusion.57), channel_id=1, source_target_pairs={{0,4},{1,5},{2,6},{3,7},{4,0},{5,1},{6,2},{7,3},{8,12},{9,13},{10,... | collective-permute-start | bytes 3080 | tf_op jit(solution)/shard_map/ppermute | solution.py:23
  131.4 10.7 %collective-permute-start.12 = (f32[16,16]{0,1:T(8,128)S(1)}, f32[16,16]{0,1:T(8,128)S(1)}, u32[]{:S(2)}, u32[]{:S(2)}) collective-permute-start(f32[16,16]{0,1:T(8,128)S(1)} %fusion.59), channel_id=1, source_target_pairs={{0,8},{1,9},{2,10},{3,11},{4,12},{5,13},{6,14},{7,15},{8,0},{9,1},... | collective-permute-start | bytes 3080 | tf_op jit(solution)/shard_map/ppermute | solution.py:23
where the time goes:
time: 153 us
  other arithmetic  43.6 us (28%)
  starting transfers between devices  42.6 us (28%)
  waiting for transfers between devices  27.5 us (18%)
  local copies, waits for them, and re-layouts  22.7 us (15%)
  matrix products  15.2 us (10%)
    ppermute x9, starting transfers between devices, from_partner(): lax.ppermute(array, axis, [(i, i ^ 1 << bit) for i in range(lax.axis_size...  31.1 us
    ppermute x9, waiting for transfers between devices, from_partner(): lax.ppermute(array, axis, [(i, i ^ 1 << bit) for i in range(lax.axis_size...  23.3 us
    another operation x27, other arithmetic, merge_factors(): return jnp.linalg.cholesky(gram).T  19.3 us
    ppermute x2, starting transfers between devices, with_halo(): lax.ppermute(lax.slice_in_dim(block, block.shape[dim] - width, None, axis...  8.26 us
    add x2, other arithmetic, cell_values(): total = total + jnp.where(material == index, table[index], jnp.float32(0.0))  7.63 us
    dot_general x9, matrix products, merge_factors(): gram = jnp.dot(upper_own.T, upper_own, precision=lax.Precision.HIGHEST)  7 us
    transpose x8, other arithmetic, merge_factors(): return jnp.linalg.cholesky(gram).T  5.19 us
    unnamed x19, local copies, waits for them, and re-layouts  5.08 us
  transfers between devices with their start and end apart: 13, of which 10 were waited for; matrix products, arithmetic and copies ran while one was open for 13% of the time, Pallas kernels for 0%

commit v1 on v0

v1 whole, which is shorter than its diff:
```python
import functools
import math

import jax
import jax.numpy as jnp
from jax import lax
from jax.experimental import pallas as pl
from jax.experimental.pallas import tpu as pltpu
from jax.sharding import PartitionSpec as P

PROBES = 16
SLABS = 24
DEPTH = 12
XS = 8
YS = 256
BLOCK = PROBES * XS
F32 = jnp.float32
BF16 = jnp.bfloat16
NT = (((1,), (1,)), ((), ()))
TN = (((0,), (0,)), ((), ()))


def iota(shape, dim):
    return lax.broadcasted_iota(jnp.int32, shape, dim)


def params():
    return pltpu.CompilerParams(vmem_limit_bytes=24 * 1024 * 1024)


def pick(material, table):
    value = jnp.where(material == 0, table[0], table[1])
    value = jnp.where(material == 2, table[2], value)
    return jnp.where(material == 3, table[3], value)


def faces_kernel(probes, x_low, x_high, y_low, y_high, wide):
    field = probes[...].astype(F32).transpose(1, 0, 2, 3).reshape(SLABS * BLOCK, YS)
    wide[0] = field[:, :128]
    wide[1] = field[:, 128:]
    for face, row in ((x_low, 0), (x_high, XS - 1)):
        for half in range(2):
            rows = wide[half, pl.ds(row, SLABS * PROBES, stride=XS), :]
            face[:, half * 128 : half * 128 + 128] = rows.astype(BF16)
    row, lane = iota((16, YS), 0), iota((16, YS), 1)
    ends = (lane == jnp.where(row == 0, 0, YS - 1)) & (row < 2)
    sides = lax.dot_general(ends.astype(BF16), field.astype(BF16), NT, preferred_element_type=F32)
    y_low[...] = sides[0:1]
    y_high[...] = sides[1:2]


def faces(probes):
    return pl.pallas_call(
        faces_kernel,
        out_shape=[jax.ShapeDtypeStruct((SLABS * PROBES, YS), BF16)] * 2
        + [jax.ShapeDtypeStruct((1, SLABS * BLOCK), F32)] * 2,
        scratch_shapes=[pltpu.VMEM((2, SLABS * BLOCK, 128), F32)],
        compiler_params=params(),
        name="faces",
    )(probes)


def inner_kernel(probes, material, flow, visc_table, brink_table, cond_table, image, visc, brink, cond):
    kind = material[...]
    visc[...] = pick(kind, visc_table)
    brink[...] = pick(kind, brink_table)
    cond[...] = pick(kind, cond_table)
    row, lane = iota((YS, YS), 0), iota((YS, YS), 1)
    along_y = jnp.where(row == lane, 6.0, jnp.where(jnp.abs(row - lane) == 1, -1.0, 0.0)).astype(BF16)
    rows = SLABS * XS
    row, lane = iota((rows, rows), 0), iota((rows, rows), 1)
    along_x = jnp.where((jnp.abs(row - lane) == 1) & (row // XS == lane // XS), -1.0, 0.0).astype(BF16)

    def step(probe, carry):
        wide = probes[probe].astype(F32)
        packed = wide.reshape(rows, YS).astype(BF16)
        lap = jnp.dot(packed, along_y, preferred_element_type=F32)
        lap = lap + jnp.dot(along_x, packed, preferred_element_type=F32)
        lap = lap.reshape(SLABS, XS, YS)
        none = jnp.zeros((1, XS, YS), F32)

        def vertical(field):
            below = jnp.concatenate([none, field[:-1]], axis=0)
            above = jnp.concatenate([field[1:], none], axis=0)
            return below, above

        w, t = wide[:DEPTH], wide[DEPTH:]
        w_below, w_above = vertical(w)
        t_below, t_above = vertical(t)
        w_lap = lap[:DEPTH] - (w_below + w_above)
        t_lap = lap[DEPTH:] - (t_below + t_above)
        image[probe, :DEPTH] = visc[...] * w_lap + brink[...] * w - t
        image[probe, DEPTH:] = cond[...] * t_lap + 0.5 * w + flow[...] * (t - t_below)
        return carry

    lax.fori_loop(0, PROBES, step, 0)


def inner(probes, material, flow, tables):
    whole = pl.BlockSpec(memory_space=pltpu.VMEM)
    small = pl.BlockSpec(memory_space=pltpu.SMEM)
    cells = (DEPTH, XS, YS)
    return pl.pallas_call(
        inner_kernel,
        out_shape=pltpu.VMEM((PROBES, SLABS, XS, YS), F32),
        in_specs=[whole, whole, whole, small, small, small],
        out_specs=whole,
        scratch_shapes=[pltpu.VMEM(cells, F32)] * 3,
        compiler_params=params(),
        cost_estimate=pl.CostEstimate(flops=800_000_000, bytes_accessed=5_000_000, transcendentals=0),
        name="inner",
    )(probes, material, flow, *tables)


def gram_kernel(image, x_low, x_high, y_low, y_high, material, visc_table, cond_table, parts, gram, total):
    row, lane = iota((BLOCK, 2 * PROBES), 0), iota((BLOCK, 2 * PROBES), 1)
    at_low = (row % XS == 0) & (lane == row // XS)
    at_high = (row % XS == XS - 1) & (lane == row // XS + PROBES)
    place = jnp.where(at_low | at_high, 1.0, 0.0).astype(BF16)
    row, lane = iota((16, YS), 0), iota((16, YS), 1)
    ends = ((lane == jnp.where(row == 0, 0, YS - 1)) & (row < 2)).astype(BF16)
    side = iota((16, BLOCK), 0)
    for slab in range(SLABS):
        table = visc_table if slab < DEPTH else cond_table
        factor = pick(material[slab % DEPTH], table)
        span = pl.ds(slab * PROBES, PROBES)
        edges = jnp.concatenate([x_low[span, :], x_high[span, :]], axis=0)
        halo = jnp.dot(place, edges, preferred_element_type=F32)
        cells = pl.ds(slab * BLOCK, BLOCK)
        columns = jnp.where(side == 0, y_low[:, cells], jnp.where(side == 1, y_high[:, cells], 0.0))
        halo = halo + lax.dot_general(columns.astype(BF16), ends, TN, preferred_element_type=F32)
        full = image[:, slab] - factor[None] * halo.reshape(PROBES, XS, YS)
        full = full.reshape(BLOCK, YS)
        high = full.astype(BF16)
        low = (full - high.astype(F32)).astype(BF16)
        both = jnp.concatenate([high, low], axis=0)
        parts[slab] = both
        product = lax.dot_general(both, both, NT, preferred_element_type=F32)
        if slab == 0:
            total[...] = product
        else:
            total[...] += product
    square = total[:BLOCK, :BLOCK] + total[BLOCK:, :BLOCK] + total[:BLOCK, BLOCK:] + total[BLOCK:, BLOCK:]
    row, lane = iota((BLOCK, BLOCK), 0), iota((BLOCK, BLOCK), 1)
    square = jnp.where(row % XS == lane % XS, square, 0.0)
    square = jnp.sum(square.reshape(PROBES, XS, BLOCK), axis=1)
    top, bottom = square[:8], square[8:]
    first = iota((8, BLOCK), 1) % XS < XS // 2
    top = top + pltpu.roll(top, BLOCK - XS // 2, 1)
    bottom = bottom + pltpu.roll(bottom, XS // 2, 1)
    gram[...] = jnp.where(first, top, bottom)


def gram(image, halos, material, visc_table, cond_table):
    whole = pl.BlockSpec(memory_space=pltpu.VMEM)
    small = pl.BlockSpec(memory_space=pltpu.SMEM)
    return pl.pallas_call(
        gram_kernel,
        out_shape=[
            pltpu.VMEM((SLABS, 2 * BLOCK, YS), BF16),
            jax.ShapeDtypeStruct((8, BLOCK), F32),
        ],
        in_specs=[whole] * 6 + [small] * 2,
        out_specs=[whole] * 2,
        scratch_shapes=[pltpu.VMEM((2 * BLOCK, 2 * BLOCK), F32)],
        compiler_params=params(),
        name="gram",
    )(image, *halos, material, visc_table, cond_table)


CHUNK = 4


def basis_kernel(scale, parts, pieces, basis, factor, result, sems):
    shape = (PROBES, BLOCK)
    row, lane = iota(shape, 0), iota(shape, 1)
    half = jnp.sum(pieces[...], axis=0)
    lane8 = iota((8, BLOCK), 1)
    for step in (1, 2):
        ahead = pltpu.roll(half, BLOCK - step, 1)
        behind = pltpu.roll(half, step, 1)
        half = half + jnp.where(lane8 & step == 0, ahead, behind)
    first = lane8 % XS < XS // 2
    top = jnp.where(first, half, pltpu.roll(half, XS // 2, 1))
    bottom = jnp.where(first, pltpu.roll(half, BLOCK - XS // 2, 1), half)
    left = jnp.concatenate([top, bottom], axis=0)
    right = jnp.where(lane // XS == row, 1.0, 0.0).astype(F32)
    pivots = jnp.ones(shape, F32)
    for k in range(PROBES):
        column = jnp.broadcast_to(left[:, k * XS : k * XS + 1], shape)
        pivot = jnp.broadcast_to(column[k : k + 1], shape)
        pivots = jnp.where(row == k, pivot, pivots)
        if k + 1 < PROBES:
            ratio = jnp.where(row > k, column / pivot, 0.0)
            left = left - ratio * jnp.broadcast_to(left[k : k + 1], shape)
            right = right - ratio * jnp.broadcast_to(right[k : k + 1], shape)
    root = lax.rsqrt(pivots)
    root = root * (1.5 - 0.5 * pivots * root * root)
    right = right * (root * scale)
    mask = jnp.where(iota((XS, BLOCK), 1) % XS == iota((XS, BLOCK), 0), 1.0, 0.0)
    weight = jnp.concatenate([mask * right[q : q + 1] for q in range(PROBES)], axis=0)
    high = weight.astype(BF16)
    low = (weight - high.astype(F32)).astype(BF16)
    weight = jnp.concatenate(
        [jnp.concatenate([high, high], axis=1), jnp.concatenate([low, low], axis=1)], axis=0
    )

    copies = []
    for slab in range(SLABS):
        out = jnp.dot(weight, parts[slab], preferred_element_type=F32)
        out = out[:BLOCK] + out[BLOCK:]
        result[:, slab] = out.reshape(PROBES, XS, YS)
        if slab % CHUNK == CHUNK - 1:
            span = pl.ds(slab - CHUNK + 1, CHUNK)
            copy = pltpu.make_async_copy(result.at[:, span], basis.at[:, span], sems.at[slab // CHUNK])
            copy.start()
            copies.append(copy)
    upper = jnp.where(lane // XS >= row, left * (root * (1.0 / scale)), 0.0)
    chosen = jnp.where(iota((BLOCK, PROBES), 0) == XS * iota((BLOCK, PROBES), 1), 1.0, 0.0)
    factor[...] = jnp.dot(upper, chosen, precision=lax.Precision.HIGHEST, preferred_element_type=F32)
    for copy in copies:
        copy.wait()


def orthonormal(parts, pieces, scale):
    whole = pl.BlockSpec(memory_space=pltpu.VMEM)
    return pl.pallas_call(
        functools.partial(basis_kernel, scale),
        out_shape=[
            jax.ShapeDtypeStruct((PROBES, SLABS, XS, YS), F32),
            jax.ShapeDtypeStruct((PROBES, PROBES), F32),
        ],
        in_specs=[whole, whole],
        out_specs=[pl.BlockSpec(memory_space=pl.ANY), whole],
        scratch_shapes=[
            pltpu.VMEM((PROBES, SLABS, XS, YS), F32),
            pltpu.SemaphoreType.DMA((SLABS // CHUNK,)),
        ],
        compiler_params=params(),
        name="orthonormal",
    )(parts, pieces)


def shift(array, axis, by):
    count = lax.axis_size(axis)
    return lax.ppermute(array, axis, [(i, i + by) for i in range(count) if 0 <= i + by < count])


def all_copies(array, axis):
    copies = jnp.broadcast_to(array[None], (lax.axis_size(axis),) + array.shape)
    return lax.all_to_all(copies, axis, 0, 0)


def on_device(probes, material, visc_table, brink_table, cond_table, base_flow):
    shape = probes.shape
    probes = probes.reshape(PROBES, SLABS, XS, YS)
    x_low, x_high, y_low, y_high = faces(probes)
    halos = (shift(x_high, "gx", 1), shift(x_low, "gx", -1), shift(y_high, "gy", 1), shift(y_low, "gy", -1))
    image = inner(probes, material, base_flow, (visc_table, brink_table, cond_table))
    parts, local = gram(image, halos, material, visc_table, cond_table)
    slab_sum = jnp.sum(all_copies(local, "gy"), axis=0)
    pieces = all_copies(slab_sum, "gx")
    rows_total = SLABS * XS * YS * lax.axis_size("gx") * lax.axis_size("gy")
    basis, factor = orthonormal(parts, pieces, math.sqrt(rows_total))
    return (basis.reshape(shape), factor)


def solution(mesh):
    grid = P(None, "gx", "gy")
    in_specs = (P(None, None, None, "gx", "gy"), grid, P(), P(), P(), grid)
    out_specs = (P(None, None, None, "gx", "gy"), P())
    return jax.shard_map(
        on_device, mesh=mesh, in_specs=in_specs, out_specs=out_specs, check_vma=False
    )
```

time: 153 us -> 70.5 us (0.46)
  the two profiles are of different devices: /device:TPU:30 before, /device:TPU:1 now
where the time goes in v1:
time: 70.5 us; the launch traced here: 70.1 us
  blocking collectives  39.5 us (56%)
  starting transfers between devices  12.7 us (18%)
  Pallas kernels  12 us (17%)
  local copies, waits for them, and re-layouts  5.17 us (7%)
  between operations  0.73 us (1%)
    all_to_all x2, blocking collectives, all_copies(): return lax.all_to_all(copies, axis, 0, 0)  39.5 us
    ppermute x4, starting transfers between devices, shift(): lax.ppermute(array, axis, [(i, i + by) for i in range(count) if 0 <= i +...  12.7 us
    unnamed x12, local copies, waits for them, and re-layouts  5.15 us
    pallas_call x1, Pallas kernels, orthonormal(): pl.pallas_call(functools.partial(basis_kernel, scale), out_shape=[jax.Sha...  4.55 us
    pallas_call x1, Pallas kernels, inner(): pl.pallas_call(inner_kernel, out_shape=pltpu.VMEM((PROBES, SLABS, XS, YS)...  4.21 us
    pallas_call x1, Pallas kernels, gram(): pl.pallas_call(gram_kernel, out_shape=[pltpu.VMEM((SLABS, 2 * BLOCK, YS),...  2.66 us
  transfers between devices with their start and end apart: 4, of which 0 were waited for; matrix products, arithmetic and copies ran while one was open for 0% of the time, Pallas kernels for 6%

profile of v1, /device:TPU:1, one launch (start us, length us, event | category | flops | bytes accessed | tf_op | source)
XLA Modules:
  0.0 70.1 jit_solution(12859093334670419881)
XLA Ops:
  0.6 0.0 copy-start
  0.6 1.4 %copy-done = bf16[16,2,12,8,256]{4,3,2,1,0:T(8,128)(2,1)S(1)} copy-done((bf16[16,2,12,8,256]{4,3,2,1,0:T(8,128)(2,1)S(1)}, bf16[16,2,12,8,256]{4,3,2,1,0:T(8,128)(2,1)}, u32[]{:S(2)}) %copy-start) | copy-done | bytes 1572888
  2.0 0.6 faces.1
  2.6 4.0 %collective-permute-start = (bf16[384,256]{1,0:T(8,128)(2,1)S(1)}, bf16[384,256]{1,0:T(8,128)(2,1)S(1)}, u32[]{:S(2)}, u32[]{:S(2)}) collective-permute-start(bf16[384,256]{1,0:T(8,128)(2,1)S(1)} %get-tuple-element.10), channel_id=1, source_target_pairs={{0,16},{16,32},{32,48},{48,64},{64,80},{80,96},{96,112},{112,128},... | collective-permute-start | bytes 589832 | tf_op jit(solution)/shard_map/ppermute | solution.py:246
  6.6 1.3 %collective-permute-start.1 = (bf16[384,256]{1,0:T(8,128)(2,1)S(1)}, bf16[384,256]{1,0:T(8,128)(2,1)S(1)}, u32[]{:S(2)}, u32[]{:S(2)}) collective-permute-start(bf16[384,256]{1,0:T(8,128)(2,1)S(1)} %get-tuple-element.11), channel_id=1, source_target_pairs={{16,0},{32,16},{48,32},{64,48},{80,64},{96,80},{112,96},{128,112},... | collective-permute-start | bytes 589832 | tf_op jit(solution)/shard_map/ppermute | solution.py:246
  7.9 4.8 %collective-permute-start.2 = (f32[1,3072]{1,0:T(1,128)S(1)}, f32[1,3072]{1,0:T(1,128)S(1)}, u32[]{:S(2)}, u32[]{:S(2)}) collective-permute-start(f32[1,3072]{1,0:T(1,128)S(1)} %get-tuple-element.12), channel_id=1, source_target_pairs={{0,1},{1,2},{2,3},{3,4},{4,5},{5,6},{6,7},{7,8},{8,9},{9,10},{10,1... | collective-permute-start | bytes 36872 | tf_op jit(solution)/shard_map/ppermute | solution.py:246
  12.8 2.6 %collective-permute-start.3 = (f32[1,3072]{1,0:T(1,128)S(1)}, f32[1,3072]{1,0:T(1,128)S(1)}, u32[]{:S(2)}, u32[]{:S(2)}) collective-permute-start(f32[1,3072]{1,0:T(1,128)S(1)} %get-tuple-element.13), channel_id=1, source_target_pairs={{1,0},{2,1},{3,2},{4,3},{5,4},{6,5},{7,6},{8,7},{9,8},{10,9},{11,1... | collective-permute-start | bytes 36872 | tf_op jit(solution)/shard_map/ppermute | solution.py:246
  15.4 0.0 copy-start.1
  15.4 0.9 %copy-done.1 = s32[12,8,256]{2,1,0:T(8,128)S(1)} copy-done((s32[12,8,256]{2,1,0:T(8,128)S(1)}, s32[12,8,256]{2,1,0:T(8,128)}, u32[]{:S(2)}) %copy-start.1) | copy-done | bytes 98328
  16.3 0.0 copy-start.2
  16.3 0.9 %copy-done.2 = f32[12,8,256]{2,1,0:T(8,128)S(1)} copy-done((f32[12,8,256]{2,1,0:T(8,128)S(1)}, f32[12,8,256]{2,1,0:T(8,128)}, u32[]{:S(2)}) %copy-start.2) | copy-done | bytes 98328
  17.1 0.0 copy-start.3
  17.1 0.7 copy-done.3
  17.8 0.7 copy-done.4
  18.5 0.7 copy-done.5
  19.1 4.2 %inner.1.image = f32[16,24,8,256]{3,2,1,0:T(8,128)S(1)} custom-call(bf16[16,24,8,256]{3,2,1,0:T(8,128)(2,1)S(1)} %bitcast.3, s32[12,8,256]{2,1,0:T(8,128)S(1)} %copy-done.1, f32[12,8,256]{2,1,0:T(8,128)S(1)} %copy-done.2, f32[4]{0:T(128)S(1)} %copy-done.3, f32[4]{0:T(128)S(1)} %copy-done.5, f32[4]{0:T(128)S(1)} %copy-done.4), custom_call_target="tpu_custom_call" | custom-call | flops 800000000 | bytes 5000000 | tf_op jit(solution)/shard_map/inner/pallas_call | solution.py:103
  23.3 0.0 collective-permute-done.2.y_low
  23.3 0.0 collective-permute-done.3.y_high
  23.4 0.0 collective-permute-done.x_low
  23.4 0.0 collective-permute-done.1.x_high
  23.4 2.7 %gram.1 = (bf16[24,256,256]{2,1,0:T(8,128)(2,1)S(1)}, f32[8,128]{1,0:T(8,128)S(1)}) custom-call(f32[16,24,8,256]{3,2,1,0:T(8,128)S(1)} %inner.1.image, bf16[384,256]{1,0:T(8,128)(2,1)S(1)} %collective-permute-done.x_low, bf16[384,256]{1,0:T(8,128)(2,1)S(1)} %collective-permute-done.1.x_high, f32[1,3072]{1,0:T(1,128)S(1)} %collective-permute-done.2.y_low, ...), custom_call_target="tpu_custom_call" | custom-call | tf_op jit(solution)/shard_map/gram/pallas_call | solution.py:157
  26.0 18.2 %all_to_all.10 = f32[16,8,128]{2,1,0:T(8,128)S(1)} all-to-all(f32[16,8,128]{2,1,0:T(8,128)S(1)} %broadcast_in_dim.4), channel_id=1, replica_groups=mesh['gx'=32,'gy'=16] {'gy'}, dimensions={0} | all-to-all | bytes 131072 | tf_op jit(solution)/shard_map/all_to_all | solution.py:251
  44.3 21.3 %all_to_all.11.pieces = f32[32,8,128]{2,1,0:T(8,128)S(1)} all-to-all(f32[32,8,128]{2,1,0:T(8,128)S(1)} %broadcast_in_dim.5), channel_id=1, replica_groups=mesh['gx'=32,'gy'=16] {'gx'}, dimensions={0} | all-to-all | bytes 262144 | tf_op jit(solution)/shard_map/all_to_all | solution.py:251
  65.6 4.5 %orthonormal.1 = (f32[16,24,8,256]{3,2,1,0:T(8,128)}, f32[16,16]{1,0:T(8,128)}) custom-call(bf16[24,256,256]{2,1,0:T(8,128)(2,1)S(1)} %get-tuple-element.14.parts, f32[32,8,128]{2,1,0:T(8,128)S(1)} %all_to_all.11.pieces), custom_call_target="tpu_custom_call" | custom-call | tf_op jit(solution)/shard_map/orthonormal/pallas_call | solution.py:227
  (5 shorter events, 0.0 us)
Async XLA Ops:
  0.6 1.4 %copy-start = (bf16[16,2,12,8,256]{4,3,2,1,0:T(8,128)(2,1)S(1)}, bf16[16,2,12,8,256]{4,3,2,1,0:T(8,128)(2,1)}, u32[]{:S(2)}) copy-start(bf16[16,2,12,8,256]{4,3,2,1,0:T(8,128)(2,1)} %param.6) | copy-start | bytes 4718596
  2.6 20.7 %collective-permute-start = (bf16[384,256]{1,0:T(8,128)(2,1)S(1)}, bf16[384,256]{1,0:T(8,128)(2,1)S(1)}, u32[]{:S(2)}, u32[]{:S(2)}) collective-permute-start(bf16[384,256]{1,0:T(8,128)(2,1)S(1)} %get-tuple-element.10), channel_id=1, source_target_pairs={{0,16},{16,32},{32,48},{48,64},{64,80},{80,96},{96,112},{112,128},... | collective-permute-start | bytes 589832 | tf_op jit(solution)/shard_map/ppermute | solution.py:246
  6.6 16.8 %collective-permute-start.1 = (bf16[384,256]{1,0:T(8,128)(2,1)S(1)}, bf16[384,256]{1,0:T(8,128)(2,1)S(1)}, u32[]{:S(2)}, u32[]{:S(2)}) collective-permute-start(bf16[384,256]{1,0:T(8,128)(2,1)S(1)} %get-tuple-element.11), channel_id=1, source_target_pairs={{16,0},{32,16},{48,32},{64,48},{80,64},{96,80},{112,96},{128,112},... | collective-permute-start | bytes 589832 | tf_op jit(solution)/shard_map/ppermute | solution.py:246
  7.9 15.4 %collective-permute-start.2 = (f32[1,3072]{1,0:T(1,128)S(1)}, f32[1,3072]{1,0:T(1,128)S(1)}, u32[]{:S(2)}, u32[]{:S(2)}) collective-permute-start(f32[1,3072]{1,0:T(1,128)S(1)} %get-tuple-element.12), channel_id=1, source_target_pairs={{0,1},{1,2},{2,3},{3,4},{4,5},{5,6},{6,7},{7,8},{8,9},{9,10},{10,1... | collective-permute-start | bytes 36872 | tf_op jit(solution)/shard_map/ppermute | solution.py:246
  12.8 10.6 %collective-permute-start.3 = (f32[1,3072]{1,0:T(1,128)S(1)}, f32[1,3072]{1,0:T(1,128)S(1)}, u32[]{:S(2)}, u32[]{:S(2)}) collective-permute-start(f32[1,3072]{1,0:T(1,128)S(1)} %get-tuple-element.13), channel_id=1, source_target_pairs={{1,0},{2,1},{3,2},{4,3},{5,4},{6,5},{7,6},{8,7},{9,8},{10,9},{11,1... | collective-permute-start | bytes 36872 | tf_op jit(solution)/shard_map/ppermute | solution.py:246
  15.4 0.9 %copy-start.1 = (s32[12,8,256]{2,1,0:T(8,128)S(1)}, s32[12,8,256]{2,1,0:T(8,128)}, u32[]{:S(2)}) copy-start(s32[12,8,256]{2,1,0:T(8,128)} %material.3) | copy-start | bytes 294916
  16.3 0.9 %copy-start.2 = (f32[12,8,256]{2,1,0:T(8,128)S(1)}, f32[12,8,256]{2,1,0:T(8,128)}, u32[]{:S(2)}) copy-start(f32[12,8,256]{2,1,0:T(8,128)} %flow.1) | copy-start | bytes 294916
  17.1 0.7 copy-start.3
  17.8 0.7 copy-start.4
  18.5 0.7 copy-start.5

commit v2 on v1

v2 whole, which is shorter than its diff:
```python
import functools
import math

import jax
import jax.numpy as jnp
from jax import lax
from jax.experimental import pallas as pl
from jax.experimental.pallas import tpu as pltpu
from jax.sharding import PartitionSpec as P

PROBES = 16
SLABS = 24
DEPTH = 12
XS = 8
YS = 256
BLOCK = PROBES * XS
F32 = jnp.float32
BF16 = jnp.bfloat16
NT = (((1,), (1,)), ((), ()))
TN = (((0,), (0,)), ((), ()))


def iota(shape, dim):
    return lax.broadcasted_iota(jnp.int32, shape, dim)


def params():
    return pltpu.CompilerParams(vmem_limit_bytes=24 * 1024 * 1024)


def pick(material, table):
    value = jnp.where(material == 0, table[0], table[1])
    value = jnp.where(material == 2, table[2], value)
    return jnp.where(material == 3, table[3], value)


def first_ends(parity):
    return (XS - 1) * (1 - parity[0]), (YS - 1) * (1 - parity[1])


def parities():
    return lax.axis_index("gx") % 2, lax.axis_index("gy") % 2


LOADS = 4


def whole_rows(wide, slab):
    return jnp.concatenate([wide[0, slab], wide[1, slab]], axis=1)


def faces_kernel(
    probes, material, flow_in, visc_in, brink_in, cond_in,
    x_first, x_second, y_first, y_second, wide, flow, visc, brink, cond,
    packed, kind, visc_table, brink_table, cond_table, sems,
):
    each = PROBES // LOADS
    loads = [
        pltpu.make_async_copy(probes.at[pl.ds(i * each, each)], packed.at[pl.ds(i * each, each)], sems.at[i])
        for i in range(LOADS)
    ]
    others = ((material, kind), (visc_in, visc_table), (brink_in, brink_table), (cond_in, cond_table), (flow_in, flow))
    others = [pltpu.make_async_copy(src, dst, sems.at[LOADS + i]) for i, (src, dst) in enumerate(others)]
    for copy in loads + others:
        copy.start()
    x_end, y_end = first_ends(parities())
    for i, copy in enumerate(loads):
        copy.wait()
        for probe in range(i * each, (i + 1) * each):
            field = packed[probe].astype(F32)
            for half in range(2):
                wide[half, :, probe * XS : (probe + 1) * XS, :] = field[:, :, half * 128 : half * 128 + 128]
    rows = wide.reshape(2, SLABS * BLOCK, 128)
    for face, end in ((x_first, x_end), (x_second, XS - 1 - x_end)):
        for half in range(2):
            ends = rows[half, pl.ds(end, SLABS * PROBES, stride=XS), :]
            face[:, half * 128 : half * 128 + 128] = ends.astype(BF16)
    lane = iota((BLOCK, 128), 1)
    sides = jnp.zeros((BLOCK, 128), F32)
    for slab in range(SLABS):
        sides = jnp.where(lane == slab, pltpu.roll(wide[0, slab], slab, 1), sides)
        sides = jnp.where(lane == slab + 32, pltpu.roll(wide[1, slab], slab + 33, 1), sides)
    sides = sides.T
    low, high = sides[:32], sides[32:64]
    y_first[...] = jnp.where(y_end == 0, low, high).astype(BF16)
    y_second[...] = jnp.where(y_end == 0, high, low).astype(BF16)
    for copy in others:
        copy.wait()
    visc[...] = pick(kind[...], visc_table)
    brink[...] = pick(kind[...], brink_table)
    cond[...] = pick(kind[...], cond_table)


def faces(probes, material, flow, tables):
    cells = (DEPTH, XS, YS)
    arrays = [pltpu.with_memory_space_constraint(a, pltpu.HBM) for a in (probes, material, flow, *tables)]
    whole = pl.BlockSpec(memory_space=pltpu.VMEM)
    return pl.pallas_call(
        faces_kernel,
        out_shape=[jax.ShapeDtypeStruct((SLABS * PROBES, YS), BF16)] * 2
        + [jax.ShapeDtypeStruct((32, BLOCK), BF16)] * 2
        + [pltpu.VMEM((2, SLABS, BLOCK, 128), F32)]
        + [pltpu.VMEM(cells, F32)] * 4,
        in_specs=[pl.BlockSpec(memory_space=pl.ANY)] * 6,
        out_specs=[whole] * 9,
        scratch_shapes=[
            pltpu.VMEM((PROBES, SLABS, XS, YS), BF16),
            pltpu.VMEM(cells, jnp.int32),
            pltpu.SMEM((4,), F32),
            pltpu.SMEM((4,), F32),
            pltpu.SMEM((4,), F32),
            pltpu.SemaphoreType.DMA((LOADS + 5,)),
        ],
        compiler_params=params(),
        name="faces",
    )(*arrays)


def inner_kernel(wide, flow, visc, brink, cond, image):
    row, lane = iota((YS, YS), 0), iota((YS, YS), 1)
    along_y = jnp.where(row == lane, 6.0, jnp.where(jnp.abs(row - lane) == 1, -1.0, 0.0)).astype(BF16)
    along_x = jnp.where((jnp.abs(row - lane) == 1) & (row // XS == lane // XS), -1.0, 0.0).astype(BF16)
    block = (PROBES, XS, YS)

    def around(z):
        if z == 0:
            return whole_rows(wide, 1)
        if z == DEPTH - 1:
            return whole_rows(wide, z - 1)
        return whole_rows(wide, z - 1) + whole_rows(wide, z + 1)

    def around_t(z):
        if z == 0:
            return whole_rows(wide, DEPTH + 1)
        if z == DEPTH - 1:
            return whole_rows(wide, DEPTH + z - 1)
        return whole_rows(wide, DEPTH + z - 1) + whole_rows(wide, DEPTH + z + 1)

    for z in range(DEPTH):
        w, t = whole_rows(wide, z), whole_rows(wide, DEPTH + z)
        both = jnp.concatenate([w.astype(BF16), t.astype(BF16)], axis=0)
        lap = jnp.dot(both, along_y, preferred_element_type=F32)
        lap = lap + jnp.dot(along_x, both, preferred_element_type=F32)
        w_lap = (lap[:BLOCK] - around(z)).reshape(block)
        t_lap = (lap[BLOCK:] - around_t(z)).reshape(block)
        w3, t3 = w.reshape(block), t.reshape(block)
        rise = t3 if z == 0 else t3 - whole_rows(wide, DEPTH + z - 1).reshape(block)
        image[z] = (visc[z][None] * w_lap + brink[z][None] * w3 - t3).reshape(BLOCK, YS)
        image[DEPTH + z] = (cond[z][None] * t_lap + 0.5 * w3 + flow[z][None] * rise).reshape(BLOCK, YS)


def inner(wide, flow, visc, brink, cond):
    whole = pl.BlockSpec(memory_space=pltpu.VMEM)
    return pl.pallas_call(
        inner_kernel,
        out_shape=pltpu.VMEM((SLABS, BLOCK, YS), F32),
        in_specs=[whole] * 5,
        out_specs=whole,
        compiler_params=params(),
        cost_estimate=pl.CostEstimate(flops=800_000_000, bytes_accessed=6_000_000, transcendentals=0),
        name="inner",
    )(wide, flow, visc, brink, cond)


def gram_kernel(image, visc, cond, x_first, x_second, y_first, y_second, parts, gram, total):
    x_end, y_end = first_ends(parities())
    row, lane = iota((BLOCK, 2 * PROBES), 0), iota((BLOCK, 2 * PROBES), 1)
    target = jnp.where(lane < PROBES, x_end, XS - 1 - x_end)
    place = jnp.where((row % XS == target) & (row // XS == lane % PROBES), 1.0, 0.0).astype(BF16)
    columns = jnp.concatenate([y_first[...].astype(F32), y_second[...].astype(F32)], axis=0).T
    place = jnp.concatenate([place, columns.astype(BF16)], axis=1)
    row, lane = iota((64, YS), 0), iota((64, YS), 1)
    at_end = jnp.where(row < 32, y_end, YS - 1 - y_end) == lane
    for slab in range(SLABS):
        factor = visc[slab] if slab < DEPTH else cond[slab - DEPTH]
        span = pl.ds(slab * PROBES, PROBES)
        ends = jnp.where(at_end & (row % 32 == slab), 1.0, 0.0).astype(BF16)
        edges = jnp.concatenate([x_first[span, :], x_second[span, :], ends], axis=0)
        halo = jnp.dot(place, edges, preferred_element_type=F32).reshape(PROBES, XS, YS)
        full = image[slab] - (factor[None] * halo).reshape(BLOCK, YS)
        high = full.astype(BF16)
        parts[slab, :BLOCK] = high
        parts[slab, BLOCK:] = (full - high.astype(F32)).astype(BF16)
    for slab in range(SLABS):
        product = lax.dot_general(parts[slab], parts[slab, :BLOCK], NT, preferred_element_type=F32)
        if slab == 0:
            total[...] = product
        else:
            total[...] += product
    mixed = total[BLOCK:]
    square = total[:BLOCK] + mixed + mixed.T
    row, lane = iota((BLOCK, BLOCK), 0), iota((BLOCK, BLOCK), 1)
    square = jnp.where(row % XS == lane % XS, square, 0.0)
    square = jnp.sum(square.reshape(PROBES, XS, BLOCK), axis=1)
    top, bottom = square[:8], square[8:]
    first = iota((8, BLOCK), 1) % XS < XS // 2
    top = top + pltpu.roll(top, BLOCK - XS // 2, 1)
    bottom = bottom + pltpu.roll(bottom, XS // 2, 1)
    gram[...] = jnp.where(first, top, bottom)


def gram(image, visc, cond, halos):
    whole = pl.BlockSpec(memory_space=pltpu.VMEM)
    return pl.pallas_call(
        gram_kernel,
        out_shape=[
            pltpu.VMEM((SLABS, 2 * BLOCK, YS), BF16),
            jax.ShapeDtypeStruct((8, BLOCK), F32),
        ],
        in_specs=[whole] * 7,
        out_specs=[whole] * 2,
        scratch_shapes=[pltpu.VMEM((2 * BLOCK, BLOCK), F32)],
        compiler_params=params(),
        name="gram",
    )(image, visc, cond, *halos)


CHUNK = 4


def basis_kernel(scale, parts, pieces, basis, factor, result, sems):
    shape = (PROBES, BLOCK)
    row, lane = iota(shape, 0), iota(shape, 1)
    half = jnp.sum(pieces[...], axis=0)
    lane8 = iota((8, BLOCK), 1)
    for step in (1, 2):
        ahead = pltpu.roll(half, BLOCK - step, 1)
        behind = pltpu.roll(half, step, 1)
        half = half + jnp.where(lane8 & step == 0, ahead, behind)
    first = lane8 % XS < XS // 2
    top = jnp.where(first, half, pltpu.roll(half, XS // 2, 1))
    bottom = jnp.where(first, pltpu.roll(half, BLOCK - XS // 2, 1), half)
    left = jnp.concatenate([top, bottom], axis=0)
    right = jnp.where(lane // XS == row, 1.0, 0.0).astype(F32)
    heads, crosses, tails = (jnp.ones(shape, F32) for _ in range(3))
    for k in range(0, PROBES, 2):
        one = jnp.broadcast_to(left[:, k * XS : k * XS + 1], shape)
        two = jnp.broadcast_to(left[:, (k + 1) * XS : (k + 1) * XS + 1], shape)
        head = jnp.broadcast_to(one[k : k + 1], shape)
        cross = jnp.broadcast_to(one[k + 1 : k + 2], shape)
        tail = jnp.broadcast_to(two[k + 1 : k + 2], shape)
        mine = row // 2 == k // 2
        heads = jnp.where(mine, head, heads)
        crosses = jnp.where(mine, cross, crosses)
        tails = jnp.where(mine, tail, tails)
        if k + 2 < PROBES:
            over = jnp.where(row > k + 1, 1.0 / (head * tail - cross * cross), 0.0)
            first_ratio = (tail * one - cross * two) * over
            second_ratio = (head * two - cross * one) * over
            left, right = (
                side
                - first_ratio * jnp.broadcast_to(side[k : k + 1], shape)
                - second_ratio * jnp.broadcast_to(side[k + 1 : k + 2], shape)
                for side in (left, right)
            )
    odd = row % 2 == 1
    ratio = jnp.where(odd, crosses / heads, 0.0)
    left, right = (side - ratio * pltpu.roll(side, 1, 0) for side in (left, right))
    pivots = jnp.where(odd, tails - ratio * crosses, heads)
    root = lax.rsqrt(pivots)
    root = root * (1.5 - 0.5 * pivots * root * root)
    right = right * (root * scale)
    mask = jnp.where(iota((XS, BLOCK), 1) % XS == iota((XS, BLOCK), 0), 1.0, 0.0)
    weight = jnp.concatenate([mask * right[q : q + 1] for q in range(PROBES)], axis=0)
    high = weight.astype(BF16)
    low = (weight - high.astype(F32)).astype(BF16)
    weight = jnp.concatenate(
        [jnp.concatenate([high, high], axis=1), jnp.concatenate([low, low], axis=1)], axis=0
    )

    copies = []
    for slab in range(SLABS):
        out = jnp.dot(weight, parts[slab], preferred_element_type=F32)
        out = out[:BLOCK] + out[BLOCK:]
        result[:, slab] = out.reshape(PROBES, XS, YS)
        if slab % CHUNK == CHUNK - 1:
            span = pl.ds(slab - CHUNK + 1, CHUNK)
            copy = pltpu.make_async_copy(result.at[:, span], basis.at[:, span], sems.at[slab // CHUNK])
            copy.start()
            copies.append(copy)
    upper = jnp.where(lane // XS >= row, left * (root * (1.0 / scale)), 0.0)
    chosen = jnp.where(iota((BLOCK, PROBES), 0) == XS * iota((BLOCK, PROBES), 1), 1.0, 0.0)
    factor[...] = jnp.dot(upper, chosen, precision=lax.Precision.HIGHEST, preferred_element_type=F32)
    for copy in copies:
        copy.wait()


def orthonormal(parts, pieces, scale):
    whole = pl.BlockSpec(memory_space=pltpu.VMEM)
    return pl.pallas_call(
        functools.partial(basis_kernel, scale),
        out_shape=[
            jax.ShapeDtypeStruct((PROBES, SLABS, XS, YS), F32),
            jax.ShapeDtypeStruct((PROBES, PROBES), F32),
        ],
        in_specs=[whole, whole],
        out_specs=[pl.BlockSpec(memory_space=pl.ANY), whole],
        scratch_shapes=[
            pltpu.VMEM((PROBES, SLABS, XS, YS), F32),
            pltpu.SemaphoreType.DMA((SLABS // CHUNK,)),
        ],
        compiler_params=params(),
        name="orthonormal",
    )(parts, pieces)


def swap(array, axis, first):
    count = lax.axis_size(axis)
    pairs = [(i, i + 1) for i in range(0 if first else 1, count - 1, 2)]
    return lax.ppermute(array, axis, pairs + [(j, i) for i, j in pairs])


def all_copies(array, axes):
    copies = jnp.broadcast_to(array[None], (lax.axis_size(axes),) + array.shape)
    return lax.all_to_all(copies, axes, 0, 0)


def on_device(probes, material, visc_table, brink_table, cond_table, base_flow):
    shape = probes.shape
    probes = probes.reshape(PROBES, SLABS, XS, YS)
    x_first, x_second, y_first, y_second, wide, flow, visc, brink, cond = faces(
        probes, material, base_flow, (visc_table, brink_table, cond_table)
    )
    halos = (
        swap(x_first, "gx", True),
        swap(x_second, "gx", False),
        swap(y_first, "gy", True),
        swap(y_second, "gy", False),
    )
    image = inner(wide, flow, visc, brink, cond)
    parts, local = gram(image, visc, cond, halos)
    slab_sum = jnp.sum(all_copies(local, "gy"), axis=0)
    pieces = all_copies(slab_sum, "gx")
    rows_total = SLABS * XS * YS * lax.axis_size("gx") * lax.axis_size("gy")
    basis, factor = orthonormal(parts, pieces, math.sqrt(rows_total))
    return (basis.reshape(shape), factor)


def solution(mesh):
    grid = P(None, "gx", "gy")
    in_specs = (P(None, None, None, "gx", "gy"), grid, P(), P(), P(), grid)
    out_specs = (P(None, None, None, "gx", "gy"), P())
    return jax.shard_map(
        on_device, mesh=mesh, in_specs=in_specs, out_specs=out_specs, check_vma=False
    )
```

time: 70.5 us -> 61.3 us (0.87)
  local copies, waits for them, and re-layouts: 5.17 us -> 0.02 us
  blocking collectives: 39.5 us -> 36.1 us
  Pallas kernels: 12 us -> 9.49 us
  waiting for transfers between devices: 0.01 us -> 1.47 us
    unnamed x12 -> x0, local copies, waits for them, and re-layouts: 5.15 us -> none
    all_to_all x2, blocking collectives: 39.5 us -> 36.1 us  [all_copies(): return lax.all_to_all(copies, axes, 0, 0)]
    pallas_call x1, Pallas kernels: 4.21 us -> 1.56 us  [inner(): pl.pallas_call(inner_kernel, out_shape=pltpu.VMEM((SLABS, BLOCK, YS), F32...]
    pallas_call x1, Pallas kernels: 0.61 us -> 2.23 us  [faces(): pl.pallas_call(faces_kernel, out_shape=[jax.ShapeDtypeStruct((SLABS * PRO...]
    ppermute x4, waiting for transfers between devices: 0.01 us -> 1.47 us  [swap(): return lax.ppermute(array, axis, pairs + [(j, i) for i, j in pairs])]
    pallas_call x1, Pallas kernels: 4.55 us -> 3.8 us  [orthonormal(): pl.pallas_call(functools.partial(basis_kernel, scale), out_shape=[jax.Sha...]
    pallas_call x1, Pallas kernels: 2.66 us -> 1.9 us  [gram(): pl.pallas_call(gram_kernel, out_shape=[pltpu.VMEM((SLABS, 2 * BLOCK, YS),...]
  transfers between devices with their start and end apart: 4 -> 4, of which waited for: 0 -> 1; matrix products, arithmetic and copies ran while one was open for 0% -> 0% of each run, Pallas kernels for 6% -> 3%
where the time goes in v2:
time: 61.3 us; the launch traced here: 61.1 us
  blocking collectives  36.1 us (59%)
  starting transfers between devices  13.3 us (22%)
  Pallas kernels  9.49 us (15%)
  waiting for transfers between devices  1.47 us (2%)
  between operations  0.69 us (1%)
    all_to_all x2, blocking collectives, all_copies(): return lax.all_to_all(copies, axes, 0, 0)  36.1 us
    ppermute x4, starting transfers between devices, swap(): return lax.ppermute(array, axis, pairs + [(j, i) for i, j in pairs])  13.3 us
    pallas_call x1, Pallas kernels, orthonormal(): pl.pallas_call(functools.partial(basis_kernel, scale), out_shape=[jax.Sha...  3.8 us
    pallas_call x1, Pallas kernels, faces(): pl.pallas_call(faces_kernel, out_shape=[jax.ShapeDtypeStruct((SLABS * PRO...  2.23 us
    pallas_call x1, Pallas kernels, gram(): pl.pallas_call(gram_kernel, out_shape=[pltpu.VMEM((SLABS, 2 * BLOCK, YS),...  1.9 us
    pallas_call x1, Pallas kernels, inner(): pl.pallas_call(inner_kernel, out_shape=pltpu.VMEM((SLABS, BLOCK, YS), F32...  1.56 us
    ppermute x4, waiting for transfers between devices, swap(): return lax.ppermute(array, axis, pairs + [(j, i) for i, j in pairs])  1.47 us
  transfers between devices with their start and end apart: 4, of which 1 were waited for; matrix products, arithmetic and copies ran while one was open for 0% of the time, Pallas kernels for 3%

profile of v2, /device:TPU:1, one launch (start us, length us, event | category | flops | bytes accessed | tf_op | source)
XLA Modules:
  0.0 61.1 jit_solution(16046276909110991171)
XLA Ops:
  0.6 2.2 %faces.1 = (bf16[384,256]{1,0:T(8,128)(2,1)S(1)}, bf16[384,256]{1,0:T(8,128)(2,1)S(1)}, bf16[32,128]{1,0:T(8,128)(2,1)S(1)}, bf16[32,128]{1,0:T(8,128)(2,1)S(1)}...) custom-call(bf16[16,24,8,256]{3,2,1,0:T(8,128)(2,1)} %bitcast.2, ...), custom_call_target="tpu_custom_call" | custom-call | tf_op jit(solution)/shard_map/faces/pallas_call | solution.py:98
  2.9 3.9 %collective-permute-start = (bf16[384,256]{1,0:T(8,128)(2,1)S(1)}, bf16[384,256]{1,0:T(8,128)(2,1)S(1)}, u32[]{:S(2)}, u32[]{:S(2)}) collective-permute-start(bf16[384,256]{1,0:T(8,128)(2,1)S(1)} %get-tuple-element.20), channel_id=1, source_target_pairs={{0,16},{32,48},{64,80},{96,112},{128,144},{160,176},{192,208},{224... | collective-permute-start | bytes 589832 | tf_op jit(solution)/shard_map/ppermute | solution.py:310
  6.8 0.7 %collective-permute-start.1 = (bf16[384,256]{1,0:T(8,128)(2,1)S(1)}, bf16[384,256]{1,0:T(8,128)(2,1)S(1)}, u32[]{:S(2)}, u32[]{:S(2)}) collective-permute-start(bf16[384,256]{1,0:T(8,128)(2,1)S(1)} %get-tuple-element.21), channel_id=1, source_target_pairs={{16,32},{48,64},{80,96},{112,128},{144,160},{176,192},{208,224},{2... | collective-permute-start | bytes 589832 | tf_op jit(solution)/shard_map/ppermute | solution.py:310
  7.5 6.8 %collective-permute-start.2 = (bf16[32,128]{1,0:T(8,128)(2,1)S(1)}, bf16[32,128]{1,0:T(8,128)(2,1)S(1)}, u32[]{:S(2)}, u32[]{:S(2)}) collective-permute-start(bf16[32,128]{1,0:T(8,128)(2,1)S(1)} %get-tuple-element.22), channel_id=1, source_target_pairs={{0,1},{2,3},{4,5},{6,7},{8,9},{10,11},{12,13},{14,15},{1,0},{3,2},... | collective-permute-start | bytes 24584 | tf_op jit(solution)/shard_map/ppermute | solution.py:310
  14.3 1.9 %collective-permute-start.3 = (bf16[32,128]{1,0:T(8,128)(2,1)S(1)}, bf16[32,128]{1,0:T(8,128)(2,1)S(1)}, u32[]{:S(2)}, u32[]{:S(2)}) collective-permute-start(bf16[32,128]{1,0:T(8,128)(2,1)S(1)} %get-tuple-element.23), channel_id=1, source_target_pairs={{1,2},{3,4},{5,6},{7,8},{9,10},{11,12},{13,14},{2,1},{4,3},{6,5},{... | collective-permute-start | bytes 24584 | tf_op jit(solution)/shard_map/ppermute | solution.py:310
  16.2 1.6 %inner.1.image = f32[24,128,256]{2,1,0:T(8,128)S(1)} custom-call(f32[2,24,128,128]{3,2,1,0:T(8,128)S(1)} %get-tuple-element.15.wide, f32[12,8,256]{2,1,0:T(8,128)S(1)} %get-tuple-element.16.flow, f32[12,8,256]{2,1,0:T(8,128)S(1)} %get-tuple-element.17.visc, f32[12,8,256]{2,1,0:T(8,128)S(1)} %get-tuple-element.18.brink, f32[12,8,256]{2,1,0:T(8,128)S(1)} %get-tuple-element.19.cond), custom_call_target="tpu_custom_call" | custom-call | flops 800000000 | bytes 6000000 | tf_op jit(solution)/shard_map/inner/pallas_call | solution.py:154
  17.8 0.0 collective-permute-done.2.y_first
  17.8 1.5 %collective-permute-done.3.y_second = bf16[32,128]{1,0:T(8,128)(2,1)S(1)} collective-permute-done((bf16[32,128]{1,0:T(8,128)(2,1)S(1)}, bf16[32,128]{1,0:T(8,128)(2,1)S(1)}, u32[]{:S(2)}, u32[]{:S(2)}) %collective-permute-start.3) | collective-permute-done | bytes 8224 | tf_op jit(solution)/shard_map/ppermute | solution.py:310
  19.2 0.0 collective-permute-done.x_first
  19.2 0.0 collective-permute-done.1.x_second
  19.2 1.9 %gram.1 = (bf16[24,256,256]{2,1,0:T(8,128)(2,1)S(1)}, f32[8,128]{1,0:T(8,128)S(1)}) custom-call(f32[24,128,256]{2,1,0:T(8,128)S(1)} %inner.1.image, f32[12,8,256]{2,1,0:T(8,128)S(1)} %get-tuple-element.17.visc, f32[12,8,256]{2,1,0:T(8,128)S(1)} %get-tuple-element.19.cond, bf16[384,256]{1,0:T(8,128)(2,1)S(1)} %collective-permute-done.x_first, ...), custom_call_target="tpu_custom_call" | custom-call | tf_op jit(solution)/shard_map/gram/pallas_call | solution.py:204
  21.2 15.2 %all_to_all.10 = f32[16,8,128]{2,1,0:T(8,128)S(1)} all-to-all(f32[16,8,128]{2,1,0:T(8,128)S(1)} %broadcast_in_dim.4), channel_id=1, replica_groups=mesh['gx'=32,'gy'=16] {'gy'}, dimensions={0} | all-to-all | bytes 131072 | tf_op jit(solution)/shard_map/all_to_all | solution.py:315
  36.4 20.9 %all_to_all.11.pieces = f32[32,8,128]{2,1,0:T(8,128)S(1)} all-to-all(f32[32,8,128]{2,1,0:T(8,128)S(1)} %broadcast_in_dim.5), channel_id=1, replica_groups=mesh['gx'=32,'gy'=16] {'gx'}, dimensions={0} | all-to-all | bytes 262144 | tf_op jit(solution)/shard_map/all_to_all | solution.py:315
  57.3 3.8 %orthonormal.1 = (f32[16,24,8,256]{3,2,1,0:T(8,128)}, f32[16,16]{1,0:T(8,128)}) custom-call(bf16[24,256,256]{2,1,0:T(8,128)(2,1)S(1)} %get-tuple-element.24.parts, f32[32,8,128]{2,1,0:T(8,128)S(1)} %all_to_all.11.pieces), custom_call_target="tpu_custom_call" | custom-call | tf_op jit(solution)/shard_map/orthonormal/pallas_call | solution.py:290
  (3 shorter events, 0.0 us)
Async XLA Ops:
  2.9 16.4 %collective-permute-start = (bf16[384,256]{1,0:T(8,128)(2,1)S(1)}, bf16[384,256]{1,0:T(8,128)(2,1)S(1)}, u32[]{:S(2)}, u32[]{:S(2)}) collective-permute-start(bf16[384,256]{1,0:T(8,128)(2,1)S(1)} %get-tuple-element.20), channel_id=1, source_target_pairs={{0,16},{32,48},{64,80},{96,112},{128,144},{160,176},{192,208},{224... | collective-permute-start | bytes 589832 | tf_op jit(solution)/shard_map/ppermute | solution.py:310
  6.8 12.4 %collective-permute-start.1 = (bf16[384,256]{1,0:T(8,128)(2,1)S(1)}, bf16[384,256]{1,0:T(8,128)(2,1)S(1)}, u32[]{:S(2)}, u32[]{:S(2)}) collective-permute-start(bf16[384,256]{1,0:T(8,128)(2,1)S(1)} %get-tuple-element.21), channel_id=1, source_target_pairs={{16,32},{48,64},{80,96},{112,128},{144,160},{176,192},{208,224},{2... | collective-permute-start | bytes 589832 | tf_op jit(solution)/shard_map/ppermute | solution.py:310
  7.5 10.3 %collective-permute-start.2 = (bf16[32,128]{1,0:T(8,128)(2,1)S(1)}, bf16[32,128]{1,0:T(8,128)(2,1)S(1)}, u32[]{:S(2)}, u32[]{:S(2)}) collective-permute-start(bf16[32,128]{1,0:T(8,128)(2,1)S(1)} %get-tuple-element.22), channel_id=1, source_target_pairs={{0,1},{2,3},{4,5},{6,7},{8,9},{10,11},{12,13},{14,15},{1,0},{3,2},... | collective-permute-start | bytes 24584 | tf_op jit(solution)/shard_map/ppermute | solution.py:310
  14.3 5.0 %collective-permute-start.3 = (bf16[32,128]{1,0:T(8,128)(2,1)S(1)}, bf16[32,128]{1,0:T(8,128)(2,1)S(1)}, u32[]{:S(2)}, u32[]{:S(2)}) collective-permute-start(bf16[32,128]{1,0:T(8,128)(2,1)S(1)} %get-tuple-element.23), channel_id=1, source_target_pairs={{1,2},{3,4},{5,6},{7,8},{9,10},{11,12},{13,14},{2,1},{4,3},{6,5},{... | collective-permute-start | bytes 24584 | tf_op jit(solution)/shard_map/ppermute | solution.py:310

commit v3 on v2

--- a/solution.py
+++ b/solution.py
@@ -8,6 +8,8 @@
 from jax.experimental.pallas import tpu as pltpu
 from jax.sharding import PartitionSpec as P
 
+GX = ("y", "x")
+GY = ("z", "core")
 PROBES = 16
 SLABS = 24
 DEPTH = 12
@@ -39,7 +41,7 @@
 
 
 def parities():
-    return lax.axis_index("gx") % 2, lax.axis_index("gy") % 2
+    return lax.axis_index(GX) % 2, lax.axis_index(GY) % 2
 
 
 LOADS = 4
@@ -49,32 +51,62 @@
     return jnp.concatenate([wide[0, slab], wide[1, slab]], axis=1)
 
 
-def faces_kernel(
-    probes, material, flow_in, visc_in, brink_in, cond_in,
-    x_first, x_second, y_first, y_second, wide, flow, visc, brink, cond,
-    packed, kind, visc_table, brink_table, cond_table, sems,
-):
+def load_kernel(probes, material, flow_in, visc_in, brink_in, cond_in, x_second, wide, flow, kind, tables, packed, sems):
     each = PROBES // LOADS
     loads = [
         pltpu.make_async_copy(probes.at[pl.ds(i * each, each)], packed.at[pl.ds(i * each, each)], sems.at[i])
         for i in range(LOADS)
     ]
-    others = ((material, kind), (visc_in, visc_table), (brink_in, brink_table), (cond_in, cond_table), (flow_in, flow))
+    others = ((material, kind), (visc_in, tables.at[0]), (brink_in, tables.at[1]), (cond_in, tables.at[2]), (flow_in, flow))
     others = [pltpu.make_async_copy(src, dst, sems.at[LOADS + i]) for i, (src, dst) in enumerate(others)]
     for copy in loads + others:
         copy.start()
-    x_end, y_end = first_ends(parities())
     for i, copy in enumerate(loads):
         copy.wait()
         for probe in range(i * each, (i + 1) * each):
             field = packed[probe].astype(F32)
             for half in range(2):
                 wide[half, :, probe * XS : (probe + 1) * XS, :] = field[:, :, half * 128 : half * 128 + 128]
+    x_end, _ = first_ends(parities())
+    x_face(wide, XS - 1 - x_end, x_second)
+    for copy in others:
+        copy.wait()
+
+
+def x_face(wide, end, face):
     rows = wide.reshape(2, SLABS * BLOCK, 128)
-    for face, end in ((x_first, x_end), (x_second, XS - 1 - x_end)):
-        for half in range(2):
-            ends = rows[half, pl.ds(end, SLABS * PROBES, stride=XS), :]
-            face[:, half * 128 : half * 128 + 128] = ends.astype(BF16)
+    for half in range(2):
+        ends = rows[half, pl.ds(end, SLABS * PROBES, stride=XS), :]
+        face[:, half * 128 : half * 128 + 128] = ends.astype(BF16)
+
+
+def load(probes, material, flow, tables):
+    cells = (DEPTH, XS, YS)
+    arrays = [pltpu.with_memory_space_constraint(a, pltpu.HBM) for a in (probes, material, flow, *tables)]
+    whole = pl.BlockSpec(memory_space=pltpu.VMEM)
+    return pl.pallas_call(
+        load_kernel,
+        out_shape=[
+            pltpu.VMEM((SLABS * PROBES, YS), BF16),
+            pltpu.VMEM((2, SLABS, BLOCK, 128), F32),
+            pltpu.VMEM(cells, F32),
+            pltpu.VMEM(cells, jnp.int32),
+            pltpu.SMEM((3, 4), F32),
+        ],
+        in_specs=[pl.BlockSpec(memory_space=pl.ANY)] * 6,
+        out_specs=[whole] * 4 + [pl.BlockSpec(memory_space=pltpu.SMEM)],
+        scratch_shapes=[
+            pltpu.VMEM((PROBES, SLABS, XS, YS), BF16),
+            pltpu.SemaphoreType.DMA((LOADS + 5,)),
+        ],
+        compiler_params=params(),
+        name="load",
+    )(*arrays)
+
+
+def faces_kernel(wide, kind, tables, x_first, y_first, y_second, visc, brink, cond):
+    x_end, y_end = first_ends(parities())
+    x_face(wide, x_end, x_first)
     lane = iota((BLOCK, 128), 1)
     sides = jnp.zeros((BLOCK, 128), F32)
     for slab in range(SLABS):
@@ -84,36 +116,22 @@
     low, high = sides[:32], sides[32:64]
     y_first[...] = jnp.where(y_end == 0, low, high).astype(BF16)
     y_second[...] = jnp.where(y_end == 0, high, low).astype(BF16)
-    for copy in others:
-        copy.wait()
-    visc[...] = pick(kind[...], visc_table)
-    brink[...] = pick(kind[...], brink_table)
-    cond[...] = pick(kind[...], cond_table)
-
-
-def faces(probes, material, flow, tables):
-    cells = (DEPTH, XS, YS)
-    arrays = [pltpu.with_memory_space_constraint(a, pltpu.HBM) for a in (probes, material, flow, *tables)]
+    for i, value in enumerate((visc, brink, cond)):
+        value[...] = pick(kind[...], [tables[i, j] for j in range(4)])
+
+
+def faces(wide, kind, tables):
     whole = pl.BlockSpec(memory_space=pltpu.VMEM)
     return pl.pallas_call(
         faces_kernel,
-        out_shape=[jax.ShapeDtypeStruct((SLABS * PROBES, YS), BF16)] * 2
-        + [jax.ShapeDtypeStruct((32, BLOCK), BF16)] * 2
-        + [pltpu.VMEM((2, SLABS, BLOCK, 128), F32)]
-        + [pltpu.VMEM(cells, F32)] * 4,
-        in_specs=[pl.BlockSpec(memory_space=pl.ANY)] * 6,
-        out_specs=[whole] * 9,
-        scratch_shapes=[
-            pltpu.VMEM((PROBES, SLABS, XS, YS), BF16),
-            pltpu.VMEM(cells, jnp.int32),
-            pltpu.SMEM((4,), F32),
-            pltpu.SMEM((4,), F32),
-            pltpu.SMEM((4,), F32),
-            pltpu.SemaphoreType.DMA((LOADS + 5,)),
-        ],
+        out_shape=[pltpu.VMEM((SLABS * PROBES, YS), BF16)]
+        + [pltpu.VMEM((32, BLOCK), BF16)] * 2
+        + [pltpu.VMEM((DEPTH, XS, YS), F32)] * 3,
+        in_specs=[whole] * 2 + [pl.BlockSpec(memory_space=pltpu.SMEM)],
+        out_specs=[whole] * 6,
         compiler_params=params(),
         name="faces",
-    )(*arrays)
+    )(wide, kind, tables)
 
 
 def inner_kernel(wide, flow, visc, brink, cond, image):
@@ -162,7 +180,16 @@
     )(wide, flow, visc, brink, cond)
 
 
-def gram_kernel(image, visc, cond, x_first, x_second, y_first, y_second, parts, gram, total):
+def fold_lanes(half):
+    lane = iota((8, BLOCK), 1)
+    for step in (1, 2):
+        ahead = pltpu.roll(half, BLOCK - step, 1)
+        behind = pltpu.roll(half, step, 1)
+        half = half + jnp.where(lane & step == 0, ahead, behind)
+    return half
+
+
+def gram_kernel(image, visc, cond, x_second, x_first, y_second, y_first, parts, gram, total):
     x_end, y_end = first_ends(parities())
     row, lane = iota((BLOCK, 2 * PROBES), 0), iota((BLOCK, 2 * PROBES), 1)
     target = jnp.where(lane < PROBES, x_end, XS - 1 - x_end)
@@ -196,7 +223,12 @@
     first = iota((8, BLOCK), 1) % XS < XS // 2
     top = top + pltpu.roll(top, BLOCK - XS // 2, 1)
     bottom = bottom + pltpu.roll(bottom, XS // 2, 1)
-    gram[...] = jnp.where(first, top, bottom)
+    half = fold_lanes(jnp.where(first, top, bottom))
+    half = jnp.where(iota((8, BLOCK), 1) % 4 == iota((8, BLOCK), 0) % 4, half, 0.0)
+    half = half + pltpu.roll(half, 7, 0)
+    half = half + pltpu.roll(half, 6, 0)
+    gram[:, :BLOCK] = half[:1]
+    gram[:, BLOCK:] = half[4:5]
 
 
 def gram(image, visc, cond, halos):
@@ -205,7 +237,7 @@
         gram_kernel,
         out_shape=[
             pltpu.VMEM((SLABS, 2 * BLOCK, YS), BF16),
-            jax.ShapeDtypeStruct((8, BLOCK), F32),
+            jax.ShapeDtypeStruct((1, 2 * BLOCK), F32),
         ],
         in_specs=[whole] * 7,
         out_specs=[whole] * 2,
@@ -218,24 +250,24 @@
 CHUNK = 4
 
 
-def basis_kernel(scale, parts, pieces, basis, factor, result, sems):
+def basis_kernel(scale, parts, pieces, basis, factor, result, small, sems):
     shape = (PROBES, BLOCK)
     row, lane = iota(shape, 0), iota(shape, 1)
-    half = jnp.sum(pieces[...], axis=0)
-    lane8 = iota((8, BLOCK), 1)
-    for step in (1, 2):
-        ahead = pltpu.roll(half, BLOCK - step, 1)
-        behind = pltpu.roll(half, step, 1)
-        half = half + jnp.where(lane8 & step == 0, ahead, behind)
+    both = jnp.sum(pieces[...], axis=0)
+    lane8, row8 = iota((8, BLOCK), 1), iota((8, BLOCK), 0)
+    half = jnp.where(
+        row8 < 4, jnp.broadcast_to(both[:, :BLOCK], (8, BLOCK)), jnp.broadcast_to(both[:, BLOCK:], (8, BLOCK))
+    )
+    half = fold_lanes(jnp.where(lane8 % 4 == row8 % 4, half, 0.0))
     first = lane8 % XS < XS // 2
     top = jnp.where(first, half, pltpu.roll(half, XS // 2, 1))
     bottom = jnp.where(first, pltpu.roll(half, BLOCK - XS // 2, 1), half)
     left = jnp.concatenate([top, bottom], axis=0)
     right = jnp.where(lane // XS == row, 1.0, 0.0).astype(F32)
     heads, crosses, tails = (jnp.ones(shape, F32) for _ in range(3))
+    columns = [jnp.broadcast_to(left[:, k * XS : k * XS + 1], shape) for k in range(PROBES)]
     for k in range(0, PROBES, 2):
-        one = jnp.broadcast_to(left[:, k * XS : k * XS + 1], shape)
-        two = jnp.broadcast_to(left[:, (k + 1) * XS : (k + 1) * XS + 1], shape)
+        one, two = columns[k : k + 2]
         head = jnp.broadcast_to(one[k : k + 1], shape)
         cross = jnp.broadcast_to(one[k + 1 : k + 2], shape)
         tail = jnp.broadcast_to(two[k + 1 : k + 2], shape)
@@ -247,6 +279,12 @@
             over = jnp.where(row > k + 1, 1.0 / (head * tail - cross * cross), 0.0)
             first_ratio = (tail * one - cross * two) * over
             second_ratio = (head * two - cross * one) * over
+            for j in range(k + 2, PROBES):
+                columns[j] = (
+                    columns[j]
+                    - first_ratio * jnp.broadcast_to(one[j : j + 1], shape)
+                    - second_ratio * jnp.broadcast_to(two[j : j + 1], shape)
+                )
             left, right = (
                 side
                 - first_ratio * jnp.broadcast_to(side[k : k + 1], shape)
@@ -278,9 +316,13 @@
             copy = pltpu.make_async_copy(result.at[:, span], basis.at[:, span], sems.at[slab // CHUNK])
             copy.start()
             copies.append(copy)
-    upper = jnp.where(lane // XS >= row, left * (root * (1.0 / scale)), 0.0)
-    chosen = jnp.where(iota((BLOCK, PROBES), 0) == XS * iota((BLOCK, PROBES), 1), 1.0, 0.0)
-    factor[...] = jnp.dot(upper, chosen, precision=lax.Precision.HIGHEST, preferred_element_type=F32)
+        if slab == CHUNK:
+            upper = jnp.where(lane // XS >= row, left * (root * (1.0 / scale)), 0.0)
+            chosen = jnp.where(iota((BLOCK, PROBES), 0) == XS * iota((BLOCK, PROBES), 1), 1.0, 0.0)
+            small[...] = jnp.dot(upper, chosen, precision=lax.Precision.HIGHEST, preferred_element_type=F32)
+            copy = pltpu.make_async_copy(small, factor, sems.at[SLABS // CHUNK])
+            copy.start()
+            copies.append(copy)
     for copy in copies:
         copy.wait()
 
@@ -294,10 +336,11 @@
             jax.ShapeDtypeStruct((PROBES, PROBES), F32),
         ],
         in_specs=[whole, whole],
-        out_specs=[pl.BlockSpec(memory_space=pl.ANY), whole],
+        out_specs=[pl.BlockSpec(memory_space=pl.ANY)] * 2,
         scratch_shapes=[
             pltpu.VMEM((PROBES, SLABS, XS, YS), F32),
-            pltpu.SemaphoreType.DMA((SLABS // CHUNK,)),
+            pltpu.VMEM((PROBES, PROBES), F32),
+            pltpu.SemaphoreType.DMA((SLABS // CHUNK + 1,)),
         ],
         compiler_params=params(),
         name="orthonormal",
@@ -318,28 +361,31 @@
 def on_device(probes, material, visc_table, brink_table, cond_table, base_flow):
     shape = probes.shape
     probes = probes.reshape(PROBES, SLABS, XS, YS)
-    x_first, x_second, y_first, y_second, wide, flow, visc, brink, cond = faces(
-        probes, material, base_flow, (visc_table, brink_table, cond_table)
-    )
-    halos = (
-        swap(x_first, "gx", True),
-        swap(x_second, "gx", False),
-        swap(y_first, "gy", True),
-        swap(y_second, "gy", False),
-    )
+    x_second, wide, flow, kind, tables = load(probes, material, base_flow, (visc_table, brink_table, cond_table))
+    x_second = swap(x_second, GX, False)
+    x_first, y_first, y_second, visc, brink, cond = faces(wide, kind, tables)
+    x_first = swap(x_first, GX, True)
+    y_second = swap(y_second, GY, False)
+    y_first = swap(y_first, GY, True)
+    halos = (x_second, x_first, y_second, y_first)
     image = inner(wide, flow, visc, brink, cond)
     parts, local = gram(image, visc, cond, halos)
-    slab_sum = jnp.sum(all_copies(local, "gy"), axis=0)
-    pieces = all_copies(slab_sum, "gx")
-    rows_total = SLABS * XS * YS * lax.axis_size("gx") * lax.axis_size("gy")
+    slab_sum = jnp.sum(all_copies(local, ("y", "core")), axis=0)
+    pieces = all_copies(slab_sum, ("x", "z"))
+    rows_total = SLABS * XS * YS * lax.axis_size(GX) * lax.axis_size(GY)
     basis, factor = orthonormal(parts, pieces, math.sqrt(rows_total))
     return (basis.reshape(shape), factor)
 
 
 def solution(mesh):
-    grid = P(None, "gx", "gy")
-    in_specs = (P(None, None, None, "gx", "gy"), grid, P(), P(), P(), grid)
-    out_specs = (P(None, None, None, "gx", "gy"), P())
+    rows, columns = mesh.shape["gx"], mesh.shape["gy"]
+    wide, cores = (4 if rows % 4 == 0 else 1), (2 if columns % 2 == 0 else 1)
+    mesh = jax.sharding.Mesh(
+        mesh.devices.reshape(rows // wide, wide, columns // cores, cores), ("y", "x", "z", "core")
+    )
+    grid = P(None, GX, GY)
+    in_specs = (P(None, None, None, GX, GY), grid, P(), P(), P(), grid)
+    out_specs = (P(None, None, None, GX, GY), P())
     return jax.shard_map(
         on_device, mesh=mesh, in_specs=in_specs, out_specs=out_specs, check_vma=False
     )

time: 61.3 us -> 57.5 us (0.938)
  blocking collectives: 36.1 us -> 34.1 us
  waiting for transfers between devices: 1.47 us -> 0.01 us
  Pallas kernels: 9.49 us -> 8.2 us
  starting transfers between devices: 13.3 us -> 14.1 us
    all_to_all x2, blocking collectives: 36.1 us -> 34.1 us  [all_copies(): return lax.all_to_all(copies, axes, 0, 0)]
    ppermute x4, waiting for transfers between devices: 1.47 us -> 0.01 us  [swap(): return lax.ppermute(array, axis, pairs + [(j, i) for i, j in pairs])]
    pallas_call x1, Pallas kernels: 3.8 us -> 2.52 us  [orthonormal(): pl.pallas_call(functools.partial(basis_kernel, scale), out_shape=[jax.Sha...]
    ppermute x4, starting transfers between devices: 13.3 us -> 14.1 us  [swap(): return lax.ppermute(array, axis, pairs + [(j, i) for i, j in pairs])]
    pallas_call x1 -> x2, Pallas kernels: 2.23 us -> 2.26 us  [the longest x1 1.66 us: load(): pl.pallas_call(load_kernel, out_shape=[pltpu.VMEM((SLABS * PROBES, YS), B...]
  transfers between devices with their start and end apart: 4 -> 4, of which waited for: 1 -> 0; matrix products, arithmetic and copies ran while one was open for 0% -> 0% of each run, Pallas kernels for 3% -> 4%
where the time goes in v3:
time: 57.5 us; the launch traced here: 57.2 us
  blocking collectives  34.1 us (59%)
  starting transfers between devices  14.1 us (25%)
  Pallas kernels  8.2 us (14%)
  between operations  0.73 us (1%)
    all_to_all x2, blocking collectives, all_copies(): return lax.all_to_all(copies, axes, 0, 0)  34.1 us
    ppermute x4, starting transfers between devices, swap(): return lax.ppermute(array, axis, pairs + [(j, i) for i, j in pairs])  14.1 us
    pallas_call x1, Pallas kernels, orthonormal(): pl.pallas_call(functools.partial(basis_kernel, scale), out_shape=[jax.Sha...  2.52 us
    pallas_call x1, Pallas kernels, gram(): pl.pallas_call(gram_kernel, out_shape=[pltpu.VMEM((SLABS, 2 * BLOCK, YS),...  1.97 us
    pallas_call x1, Pallas kernels, load(): pl.pallas_call(load_kernel, out_shape=[pltpu.VMEM((SLABS * PROBES, YS), B...  1.66 us
    pallas_call x1, Pallas kernels, inner(): pl.pallas_call(inner_kernel, out_shape=pltpu.VMEM((SLABS, BLOCK, YS), F32...  1.45 us
  transfers between devices with their start and end apart: 4, of which 0 were waited for; matrix products, arithmetic and copies ran while one was open for 0% of the time, Pallas kernels for 4%

profile of v3, /device:TPU:1, one launch (start us, length us, event | category | flops | bytes accessed | tf_op | source)
XLA Modules:
  0.0 57.2 jit_solution(7272675462849635714)
XLA Ops:
  0.6 1.7 %load.1 = (bf16[384,256]{1,0:T(8,128)(2,1)S(1)}, f32[2,24,128,128]{3,2,1,0:T(8,128)S(1)}, f32[12,8,256]{2,1,0:T(8,128)S(1)}, s32[12,8,256]{2,1,0:T(8,128)S(1)}, f32[3,4]{1,0:T(4,128)S(4)}) custom-call(bf16[16,24,8,256]{3,2,1,0:T(8,128)(2,1)} %bitcast.4, s32[12,8,256]{2,1,0:T(8,128)} %material.1, f32[12,8,256]{2,1,0:T(8,128)} %flow_in.1, f32[4]{0:T(128)} %visc_in.1, ...), custom_call_target="tpu_custom_call" | custom-call | tf_op jit(solution)/shard_map/load/pallas_call | solution.py:87
  2.3 0.7 %collective-permute-start = (bf16[384,256]{1,0:T(8,128)(2,1)S(1)}, bf16[384,256]{1,0:T(8,128)(2,1)S(1)}, u32[]{:S(2)}, u32[]{:S(2)}) collective-permute-start(bf16[384,256]{1,0:T(8,128)(2,1)S(1)} %get-tuple-element.24), channel_id=1, source_target_pairs={{16,32},{48,64},{80,96},{112,128},{144,160},{176,192},{208,224},{2... | collective-permute-start | bytes 589832 | tf_op jit(solution)/shard_map/ppermute | solution.py:353
  3.0 0.6 %faces.1 = (bf16[384,256]{1,0:T(8,128)(2,1)S(1)}, bf16[32,128]{1,0:T(8,128)(2,1)S(1)}, bf16[32,128]{1,0:T(8,128)(2,1)S(1)}, f32[12,8,256]{2,1,0:T(8,128)S(1)}, f...) custom-call(f32[2,24,128,128]{3,2,1,0:T(8,128)S(1)} %get-tuple-element.17.wide, ...), custom_call_target="tpu_custom_call" | custom-call | tf_op jit(solution)/shard_map/faces/pallas_call | solution.py:125
  3.6 6.4 %collective-permute-start.1 = (bf16[384,256]{1,0:T(8,128)(2,1)S(1)}, bf16[384,256]{1,0:T(8,128)(2,1)S(1)}, u32[]{:S(2)}, u32[]{:S(2)}) collective-permute-start(bf16[384,256]{1,0:T(8,128)(2,1)S(1)} %get-tuple-element.25), channel_id=1, source_target_pairs={{0,16},{32,48},{64,80},{96,112},{128,144},{160,176},{192,208},{224... | collective-permute-start | bytes 589832 | tf_op jit(solution)/shard_map/ppermute | solution.py:353
  10.0 5.1 %collective-permute-start.2 = (bf16[32,128]{1,0:T(8,128)(2,1)S(1)}, bf16[32,128]{1,0:T(8,128)(2,1)S(1)}, u32[]{:S(2)}, u32[]{:S(2)}) collective-permute-start(bf16[32,128]{1,0:T(8,128)(2,1)S(1)} %get-tuple-element.26), channel_id=1, source_target_pairs={{1,2},{3,4},{5,6},{7,8},{9,10},{11,12},{13,14},{2,1},{4,3},{6,5},{... | collective-permute-start | bytes 24584 | tf_op jit(solution)/shard_map/ppermute | solution.py:353
  15.1 1.9 %collective-permute-start.3 = (bf16[32,128]{1,0:T(8,128)(2,1)S(1)}, bf16[32,128]{1,0:T(8,128)(2,1)S(1)}, u32[]{:S(2)}, u32[]{:S(2)}) collective-permute-start(bf16[32,128]{1,0:T(8,128)(2,1)S(1)} %get-tuple-element.27), channel_id=1, source_target_pairs={{0,1},{2,3},{4,5},{6,7},{8,9},{10,11},{12,13},{14,15},{1,0},{3,2},... | collective-permute-start | bytes 24584 | tf_op jit(solution)/shard_map/ppermute | solution.py:353
  17.0 1.4 %inner.1.image = f32[24,128,256]{2,1,0:T(8,128)S(1)} custom-call(f32[2,24,128,128]{3,2,1,0:T(8,128)S(1)} %get-tuple-element.17.wide, f32[12,8,256]{2,1,0:T(8,128)S(1)} %get-tuple-element.18.flow, f32[12,8,256]{2,1,0:T(8,128)S(1)} %get-tuple-element.21.visc, f32[12,8,256]{2,1,0:T(8,128)S(1)} %get-tuple-element.22.brink, f32[12,8,256]{2,1,0:T(8,128)S(1)} %get-tuple-element.23.cond), custom_call_target="tpu_custom_call" | custom-call | flops 800000000 | bytes 6000000 | tf_op jit(solution)/shard_map/inner/pallas_call | solution.py:172
  18.5 0.0 collective-permute-done.2.y_second
  18.5 0.0 collective-permute-done.3.y_first
  18.5 0.0 collective-permute-done.x_second
  18.5 0.0 collective-permute-done.1.x_first
  18.5 2.0 %gram.1 = (bf16[24,256,256]{2,1,0:T(8,128)(2,1)S(1)}, f32[1,256]{1,0:T(1,128)S(1)}) custom-call(f32[24,128,256]{2,1,0:T(8,128)S(1)} %inner.1.image, f32[12,8,256]{2,1,0:T(8,128)S(1)} %get-tuple-element.21.visc, f32[12,8,256]{2,1,0:T(8,128)S(1)} %get-tuple-element.23.cond, bf16[384,256]{1,0:T(8,128)(2,1)S(1)} %collective-permute-done.x_second, ...), custom_call_target="tpu_custom_call" | custom-call | tf_op jit(solution)/shard_map/gram/pallas_call | solution.py:236
  20.5 14.7 %all_to_all.10 = f32[16,1,256]{2,1,0:T(1,128)S(1)} all-to-all(f32[16,1,256]{2,1,0:T(1,128)S(1)} %broadcast_in_dim.7), channel_id=1, replica_groups=mesh['y'=8,'x'=4,'z'=8,'core'=2] {'y','core'}, dimensions={0} | all-to-all | bytes 32768 | tf_op jit(solution)/shard_map/all_to_all | solution.py:358
  35.3 19.4 %all_to_all.11.pieces = f32[32,1,256]{2,1,0:T(1,128)S(1)} all-to-all(f32[32,1,256]{2,1,0:T(1,128)S(1)} %broadcast_in_dim.16), channel_id=1, replica_groups=mesh['y'=8,'x'=4,'z'=8,'core'=2] {'x','z'}, dimensions={0} | all-to-all | bytes 65536 | tf_op jit(solution)/shard_map/all_to_all | solution.py:358
  54.7 2.5 %orthonormal.1 = (f32[16,24,8,256]{3,2,1,0:T(8,128)}, f32[16,16]{1,0:T(8,128)}) custom-call(bf16[24,256,256]{2,1,0:T(8,128)(2,1)S(1)} %get-tuple-element.28.parts, f32[32,1,256]{2,1,0:T(1,128)S(1)} %all_to_all.11.pieces), custom_call_target="tpu_custom_call" | custom-call | tf_op jit(solution)/shard_map/orthonormal/pallas_call | solution.py:332
  (3 shorter events, 0.1 us)
Async XLA Ops:
  2.3 16.2 %collective-permute-start = (bf16[384,256]{1,0:T(8,128)(2,1)S(1)}, bf16[384,256]{1,0:T(8,128)(2,1)S(1)}, u32[]{:S(2)}, u32[]{:S(2)}) collective-permute-start(bf16[384,256]{1,0:T(8,128)(2,1)S(1)} %get-tuple-element.24), channel_id=1, source_target_pairs={{16,32},{48,64},{80,96},{112,128},{144,160},{176,192},{208,224},{2... | collective-permute-start | bytes 589832 | tf_op jit(solution)/shard_map/ppermute | solution.py:353
  3.6 14.9 %collective-permute-start.1 = (bf16[384,256]{1,0:T(8,128)(2,1)S(1)}, bf16[384,256]{1,0:T(8,128)(2,1)S(1)}, u32[]{:S(2)}, u32[]{:S(2)}) collective-permute-start(bf16[384,256]{1,0:T(8,128)(2,1)S(1)} %get-tuple-element.25), channel_id=1, source_target_pairs={{0,16},{32,48},{64,80},{96,112},{128,144},{160,176},{192,208},{224... | collective-permute-start | bytes 589832 | tf_op jit(solution)/shard_map/ppermute | solution.py:353
  10.0 8.5 %collective-permute-start.2 = (bf16[32,128]{1,0:T(8,128)(2,1)S(1)}, bf16[32,128]{1,0:T(8,128)(2,1)S(1)}, u32[]{:S(2)}, u32[]{:S(2)}) collective-permute-start(bf16[32,128]{1,0:T(8,128)(2,1)S(1)} %get-tuple-element.26), channel_id=1, source_target_pairs={{1,2},{3,4},{5,6},{7,8},{9,10},{11,12},{13,14},{2,1},{4,3},{6,5},{... | collective-permute-start | bytes 24584 | tf_op jit(solution)/shard_map/ppermute | solution.py:353
  15.1 3.4 %collective-permute-start.3 = (bf16[32,128]{1,0:T(8,128)(2,1)S(1)}, bf16[32,128]{1,0:T(8,128)(2,1)S(1)}, u32[]{:S(2)}, u32[]{:S(2)}) collective-permute-start(bf16[32,128]{1,0:T(8,128)(2,1)S(1)} %get-tuple-element.27), channel_id=1, source_target_pairs={{0,1},{2,3},{4,5},{6,7},{8,9},{10,11},{12,13},{14,15},{1,0},{3,2},... | collective-permute-start | bytes 24584 | tf_op jit(solution)/shard_map/ppermute | solution.py:353

commit v4 on v3

--- a/solution.py
+++ b/solution.py
@@ -19,7 +19,6 @@
 F32 = jnp.float32
 BF16 = jnp.bfloat16
 NT = (((1,), (1,)), ((), ()))
-TN = (((0,), (0,)), ((), ()))
 
 
 def iota(shape, dim):
@@ -51,7 +50,11 @@
     return jnp.concatenate([wide[0, slab], wide[1, slab]], axis=1)
 
 
-def load_kernel(probes, material, flow_in, visc_in, brink_in, cond_in, x_second, wide, flow, kind, tables, packed, sems):
+def load_kernel(
+    probes, material, flow_in, visc_in, brink_in, cond_in,
+    x_first, x_second, y_first, y_second, wide, flow, visc, brink, cond, along_y, along_x, ends_at,
+    kind, tables, packed, columns, sems,
+):
     each = PROBES // LOADS
     loads = [
         pltpu.make_async_copy(probes.at[pl.ds(i * each, each)], packed.at[pl.ds(i * each, each)], sems.at[i])
@@ -61,16 +64,37 @@
     others = [pltpu.make_async_copy(src, dst, sems.at[LOADS + i]) for i, (src, dst) in enumerate(others)]
     for copy in loads + others:
         copy.start()
+    x_end, y_end = first_ends(parities())
+    row, lane = iota((YS, YS), 0), iota((YS, YS), 1)
+    along_y[...] = jnp.where(row == lane, 6.0, jnp.where(jnp.abs(row - lane) == 1, -1.0, 0.0)).astype(BF16)
+    along_x[...] = jnp.where((jnp.abs(row - lane) == 1) & (row // XS == lane // XS), -1.0, 0.0).astype(BF16)
+    row, lane = iota((64, YS), 0), iota((64, YS), 1)
+    at_end = jnp.where(row < 32, y_end, YS - 1 - y_end) == lane
+    for slab in range(SLABS):
+        ends_at[slab] = jnp.where(at_end & (row % 32 == slab), 1.0, 0.0).astype(BF16)
+    lane = iota((XS, 128), 1)
     for i, copy in enumerate(loads):
         copy.wait()
         for probe in range(i * each, (i + 1) * each):
             field = packed[probe].astype(F32)
-            for half in range(2):
-                wide[half, :, probe * XS : (probe + 1) * XS, :] = field[:, :, half * 128 : half * 128 + 128]
-    x_end, _ = first_ends(parities())
+            rows = slice(probe * XS, (probe + 1) * XS)
+            wide[0, :, rows, :] = field[:, :, :128]
+            wide[1, :, rows, :] = field[:, :, 128:]
+            ends = jnp.where(lane < 64, field[:, :, :128], field[:, :, 128:])
+            sides = jnp.zeros((XS, 128), F32)
+            for slab in range(SLABS):
+                sides = jnp.where(lane // 2 == slab, pltpu.roll(ends[slab], 2 * slab + 1, 1), sides)
+            columns[rows] = sides
     x_face(wide, XS - 1 - x_end, x_second)
+    x_face(wide, x_end, x_first)
+    columns[...] = columns[...].T
+    high, low = columns[pl.ds(0, 32, stride=2), :], columns[pl.ds(1, 32, stride=2), :]
+    y_first[...] = jnp.where(y_end == 0, low, high).astype(BF16)
+    y_second[...] = jnp.where(y_end == 0, high, low).astype(BF16)
     for copy in others:
         copy.wait()
+    for i, value in enumerate((visc, brink, cond)):
+        value[...] = pick(kind[...], [tables[i, j] for j in range(4)])
 
 
 def x_face(wide, end, face):
@@ -86,17 +110,19 @@
     whole = pl.BlockSpec(memory_space=pltpu.VMEM)
     return pl.pallas_call(
         load_kernel,
-        out_shape=[
-            pltpu.VMEM((SLABS * PROBES, YS), BF16),
-            pltpu.VMEM((2, SLABS, BLOCK, 128), F32),
-            pltpu.VMEM(cells, F32),
+        out_shape=[pltpu.VMEM((SLABS * PROBES, YS), BF16)] * 2
+        + [pltpu.VMEM((32, BLOCK), BF16)] * 2
+        + [pltpu.VMEM((2, SLABS, BLOCK, 128), F32)]
+        + [pltpu.VMEM(cells, F32)] * 4
+        + [pltpu.VMEM((YS, YS), BF16)] * 2
+        + [pltpu.VMEM((SLABS, 64, YS), BF16)],
+        in_specs=[pl.BlockSpec(memory_space=pl.ANY)] * 6,
+        out_specs=[whole] * 12,
+        scratch_shapes=[
             pltpu.VMEM(cells, jnp.int32),
             pltpu.SMEM((3, 4), F32),
-        ],
-        in_specs=[pl.BlockSpec(memory_space=pl.ANY)] * 6,
-        out_specs=[whole] * 4 + [pl.BlockSpec(memory_space=pltpu.SMEM)],
-        scratch_shapes=[
             pltpu.VMEM((PROBES, SLABS, XS, YS), BF16),
+            pltpu.VMEM((BLOCK, 128), F32),
             pltpu.SemaphoreType.DMA((LOADS + 5,)),
         ],
         compiler_params=params(),
@@ -104,40 +130,7 @@
     )(*arrays)
 
 
-def faces_kernel(wide, kind, tables, x_first, y_first, y_second, visc, brink, cond):
-    x_end, y_end = first_ends(parities())
-    x_face(wide, x_end, x_first)
-    lane = iota((BLOCK, 128), 1)
-    sides = jnp.zeros((BLOCK, 128), F32)
-    for slab in range(SLABS):
-        sides = jnp.where(lane == slab, pltpu.roll(wide[0, slab], slab, 1), sides)
-        sides = jnp.where(lane == slab + 32, pltpu.roll(wide[1, slab], slab + 33, 1), sides)
-    sides = sides.T
-    low, high = sides[:32], sides[32:64]
-    y_first[...] = jnp.where(y_end == 0, low, high).astype(BF16)
-    y_second[...] = jnp.where(y_end == 0, high, low).astype(BF16)
-    for i, value in enumerate((visc, brink, cond)):
-        value[...] = pick(kind[...], [tables[i, j] for j in range(4)])
-
-
-def faces(wide, kind, tables):
-    whole = pl.BlockSpec(memory_space=pltpu.VMEM)
-    return pl.pallas_call(
-        faces_kernel,
-        out_shape=[pltpu.VMEM((SLABS * PROBES, YS), BF16)]
-        + [pltpu.VMEM((32, BLOCK), BF16)] * 2
-        + [pltpu.VMEM((DEPTH, XS, YS), F32)] * 3,
-        in_specs=[whole] * 2 + [pl.BlockSpec(memory_space=pltpu.SMEM)],
-        out_specs=[whole] * 6,
-        compiler_params=params(),
-        name="faces",
-    )(wide, kind, tables)
-
-
-def inner_kernel(wide, flow, visc, brink, cond, image):
-    row, lane = iota((YS, YS), 0), iota((YS, YS), 1)
-    along_y = jnp.where(row == lane, 6.0, jnp.where(jnp.abs(row - lane) == 1, -1.0, 0.0)).astype(BF16)
-    along_x = jnp.where((jnp.abs(row - lane) == 1) & (row // XS == lane // XS), -1.0, 0.0).astype(BF16)
+def inner_kernel(wide, flow, visc, brink, cond, along_y, along_x, image):
     block = (PROBES, XS, YS)
 
     def around(z):
@@ -157,8 +150,8 @@
     for z in range(DEPTH):
         w, t = whole_rows(wide, z), whole_rows(wide, DEPTH + z)
         both = jnp.concatenate([w.astype(BF16), t.astype(BF16)], axis=0)
-        lap = jnp.dot(both, along_y, preferred_element_type=F32)
-        lap = lap + jnp.dot(along_x, both, preferred_element_type=F32)
+        lap = jnp.dot(both, along_y[...], preferred_element_type=F32)
+        lap = lap + jnp.dot(along_x[...], both, preferred_element_type=F32)
         w_lap = (lap[:BLOCK] - around(z)).reshape(block)
         t_lap = (lap[BLOCK:] - around_t(z)).reshape(block)
         w3, t3 = w.reshape(block), t.reshape(block)
@@ -167,17 +160,17 @@
         image[DEPTH + z] = (cond[z][None] * t_lap + 0.5 * w3 + flow[z][None] * rise).reshape(BLOCK, YS)
 
 
-def inner(wide, flow, visc, brink, cond):
+def inner(*arrays):
     whole = pl.BlockSpec(memory_space=pltpu.VMEM)
     return pl.pallas_call(
         inner_kernel,
         out_shape=pltpu.VMEM((SLABS, BLOCK, YS), F32),
-        in_specs=[whole] * 5,
+        in_specs=[whole] * 7,
         out_specs=whole,
         compiler_params=params(),
         cost_estimate=pl.CostEstimate(flops=800_000_000, bytes_accessed=6_000_000, transcendentals=0),
         name="inner",
-    )(wide, flow, visc, brink, cond)
+    )(*arrays)
 
 
 def fold_lanes(half):
@@ -189,20 +182,17 @@
     return half
 
 
-def gram_kernel(image, visc, cond, x_second, x_first, y_second, y_first, parts, gram, total):
-    x_end, y_end = first_ends(parities())
+def gram_kernel(image, visc, cond, ends_at, x_second, x_first, y_second, y_first, parts, gram, total):
+    x_end, _ = first_ends(parities())
     row, lane = iota((BLOCK, 2 * PROBES), 0), iota((BLOCK, 2 * PROBES), 1)
     target = jnp.where(lane < PROBES, x_end, XS - 1 - x_end)
     place = jnp.where((row % XS == target) & (row // XS == lane % PROBES), 1.0, 0.0).astype(BF16)
     columns = jnp.concatenate([y_first[...].astype(F32), y_second[...].astype(F32)], axis=0).T
     place = jnp.concatenate([place, columns.astype(BF16)], axis=1)
-    row, lane = iota((64, YS), 0), iota((64, YS), 1)
-    at_end = jnp.where(row < 32, y_end, YS - 1 - y_end) == lane
     for slab in range(SLABS):
         factor = visc[slab] if slab < DEPTH else cond[slab - DEPTH]
         span = pl.ds(slab * PROBES, PROBES)
-        ends = jnp.where(at_end & (row % 32 == slab), 1.0, 0.0).astype(BF16)
-        edges = jnp.concatenate([x_first[span, :], x_second[span, :], ends], axis=0)
+        edges = jnp.concatenate([x_first[span, :], x_second[span, :], ends_at[slab]], axis=0)
         halo = jnp.dot(place, edges, preferred_element_type=F32).reshape(PROBES, XS, YS)
         full = image[slab] - (factor[None] * halo).reshape(BLOCK, YS)
         high = full.astype(BF16)
@@ -231,7 +221,7 @@
     gram[:, BLOCK:] = half[4:5]
 
 
-def gram(image, visc, cond, halos):
+def gram(image, visc, cond, ends_at, halos):
     whole = pl.BlockSpec(memory_space=pltpu.VMEM)
     return pl.pallas_call(
         gram_kernel,
@@ -239,12 +229,12 @@
             pltpu.VMEM((SLABS, 2 * BLOCK, YS), BF16),
             jax.ShapeDtypeStruct((1, 2 * BLOCK), F32),
         ],
-        in_specs=[whole] * 7,
+        in_specs=[whole] * 8,
         out_specs=[whole] * 2,
         scratch_shapes=[pltpu.VMEM((2 * BLOCK, BLOCK), F32)],
         compiler_params=params(),
         name="gram",
-    )(image, visc, cond, *halos)
+    )(image, visc, cond, ends_at, *halos)
 
 
 CHUNK = 4
@@ -361,17 +351,18 @@
 def on_device(probes, material, visc_table, brink_table, cond_table, base_flow):
     shape = probes.shape
     probes = probes.reshape(PROBES, SLABS, XS, YS)
-    x_second, wide, flow, kind, tables = load(probes, material, base_flow, (visc_table, brink_table, cond_table))
+    x_first, x_second, y_first, y_second, wide, flow, visc, brink, cond, along_y, along_x, ends_at = load(
+        probes, material, base_flow, (visc_table, brink_table, cond_table)
+    )
     x_second = swap(x_second, GX, False)
-    x_first, y_first, y_second, visc, brink, cond = faces(wide, kind, tables)
     x_first = swap(x_first, GX, True)
     y_second = swap(y_second, GY, False)
     y_first = swap(y_first, GY, True)
     halos = (x_second, x_first, y_second, y_first)
-    image = inner(wide, flow, visc, brink, cond)
-    parts, local = gram(image, visc, cond, halos)
-    slab_sum = jnp.sum(all_copies(local, ("y", "core")), axis=0)
-    pieces = all_copies(slab_sum, ("x", "z"))
+    image = inner(wide, flow, visc, brink, cond, along_y, along_x)
+    parts, local = gram(image, visc, cond, ends_at, halos)
+    slab_sum = jnp.sum(all_copies(local, ("core", "y")), axis=0)
+    pieces = all_copies(slab_sum, ("z", "x"))
     rows_total = SLABS * XS * YS * lax.axis_size(GX) * lax.axis_size(GY)
     basis, factor = orthonormal(parts, pieces, math.sqrt(rows_total))
     return (basis.reshape(shape), factor)

time: 57.5 us -> 57 us (level)
    pallas_call x1 -> x0, Pallas kernels: 0.59 us -> none  [faces(): pl.pallas_call(faces_kernel, out_shape=[pltpu.VMEM((SLABS * PROBES, YS),...]
  transfers between devices with their start and end apart: 4 -> 4, of which waited for: 0 -> 0; matrix products, arithmetic and copies ran while one was open for 0% -> 0% of each run, Pallas kernels for 4% -> 3%
where the time goes in v4:
time: 57 us; the launch traced here: 56.7 us
  blocking collectives  33.7 us (59%)
  starting transfers between devices  14.1 us (25%)
  Pallas kernels  8.09 us (14%)
  between operations  0.72 us (1%)
    all_to_all x2, blocking collectives, all_copies(): return lax.all_to_all(copies, axes, 0, 0)  33.7 us
    ppermute x4, starting transfers between devices, swap(): return lax.ppermute(array, axis, pairs + [(j, i) for i, j in pairs])  14.1 us
    pallas_call x1, Pallas kernels, orthonormal(): pl.pallas_call(functools.partial(basis_kernel, scale), out_shape=[jax.Sha...  2.52 us
    pallas_call x1, Pallas kernels, load(): pl.pallas_call(load_kernel, out_shape=[pltpu.VMEM((SLABS * PROBES, YS), B...  2.03 us
    pallas_call x1, Pallas kernels, gram(): pl.pallas_call(gram_kernel, out_shape=[pltpu.VMEM((SLABS, 2 * BLOCK, YS),...  1.93 us
    pallas_call x1, Pallas kernels, inner(): pl.pallas_call(inner_kernel, out_shape=pltpu.VMEM((SLABS, BLOCK, YS), F32...  1.61 us
  transfers between devices with their start and end apart: 4, of which 0 were waited for; matrix products, arithmetic and copies ran while one was open for 0% of the time, Pallas kernels for 3%

profile of v4, /device:TPU:1, one launch (start us, length us, event | category | flops | bytes accessed | tf_op | source)
XLA Modules:
  0.0 56.7 jit_solution(13839053114713357537)
XLA Ops:
  0.6 2.0 %load.1 = (bf16[384,256]{1,0:T(8,128)(2,1)S(1)}, bf16[384,256]{1,0:T(8,128)(2,1)S(1)}, bf16[32,128]{1,0:T(8,128)(2,1)S(1)}, bf16[32,128]{1,0:T(8,128)(2,1)S(1)},...) custom-call(bf16[16,24,8,256]{3,2,1,0:T(8,128)(2,1)} %bitcast.4, ...), custom_call_target="tpu_custom_call" | custom-call | tf_op jit(solution)/shard_map/load/pallas_call | solution.py:111
  2.7 0.7 %collective-permute-start = (bf16[384,256]{1,0:T(8,128)(2,1)S(1)}, bf16[384,256]{1,0:T(8,128)(2,1)S(1)}, u32[]{:S(2)}, u32[]{:S(2)}) collective-permute-start(bf16[384,256]{1,0:T(8,128)(2,1)S(1)} %get-tuple-element.26), channel_id=1, source_target_pairs={{16,32},{48,64},{80,96},{112,128},{144,160},{176,192},{208,224},{2... | collective-permute-start | bytes 589832 | tf_op jit(solution)/shard_map/ppermute | solution.py:343
  3.4 6.4 %collective-permute-start.1 = (bf16[384,256]{1,0:T(8,128)(2,1)S(1)}, bf16[384,256]{1,0:T(8,128)(2,1)S(1)}, u32[]{:S(2)}, u32[]{:S(2)}) collective-permute-start(bf16[384,256]{1,0:T(8,128)(2,1)S(1)} %get-tuple-element.27), channel_id=1, source_target_pairs={{0,16},{32,48},{64,80},{96,112},{128,144},{160,176},{192,208},{224... | collective-permute-start | bytes 589832 | tf_op jit(solution)/shard_map/ppermute | solution.py:343
  9.8 5.1 %collective-permute-start.2 = (bf16[32,128]{1,0:T(8,128)(2,1)S(1)}, bf16[32,128]{1,0:T(8,128)(2,1)S(1)}, u32[]{:S(2)}, u32[]{:S(2)}) collective-permute-start(bf16[32,128]{1,0:T(8,128)(2,1)S(1)} %get-tuple-element.28), channel_id=1, source_target_pairs={{1,2},{3,4},{5,6},{7,8},{9,10},{11,12},{13,14},{2,1},{4,3},{6,5},{... | collective-permute-start | bytes 24584 | tf_op jit(solution)/shard_map/ppermute | solution.py:343
  14.9 1.9 %collective-permute-start.3 = (bf16[32,128]{1,0:T(8,128)(2,1)S(1)}, bf16[32,128]{1,0:T(8,128)(2,1)S(1)}, u32[]{:S(2)}, u32[]{:S(2)}) collective-permute-start(bf16[32,128]{1,0:T(8,128)(2,1)S(1)} %get-tuple-element.29), channel_id=1, source_target_pairs={{0,1},{2,3},{4,5},{6,7},{8,9},{10,11},{12,13},{14,15},{1,0},{3,2},... | collective-permute-start | bytes 24584 | tf_op jit(solution)/shard_map/ppermute | solution.py:343
  16.8 1.6 %inner.1.image = f32[24,128,256]{2,1,0:T(8,128)S(1)} custom-call(f32[2,24,128,128]{3,2,1,0:T(8,128)S(1)} %get-tuple-element.18.wide, f32[12,8,256]{2,1,0:T(8,128)S(1)} %get-tuple-element.19.flow, f32[12,8,256]{2,1,0:T(8,128)S(1)} %get-tuple-element.20.visc, f32[12,8,256]{2,1,0:T(8,128)S(1)} %get-tuple-element.21.brink, ...), custom_call_target="tpu_custom_call" | custom-call | flops 800000000 | bytes 6000000 | tf_op jit(solution)/shard_map/inner/pallas_call | solution.py:165
  18.4 0.0 collective-permute-done.2.y_second
  18.4 0.0 collective-permute-done.3.y_first
  18.4 0.0 collective-permute-done.x_second
  18.5 0.0 collective-permute-done.1.x_first
  18.5 1.9 %gram.1 = (bf16[24,256,256]{2,1,0:T(8,128)(2,1)S(1)}, f32[1,256]{1,0:T(1,128)S(1)}) custom-call(f32[24,128,256]{2,1,0:T(8,128)S(1)} %inner.1.image, f32[12,8,256]{2,1,0:T(8,128)S(1)} %get-tuple-element.20.visc, f32[12,8,256]{2,1,0:T(8,128)S(1)} %get-tuple-element.22.cond, bf16[24,64,256]{2,1,0:T(8,128)(2,1)S(1)} %get-tuple-element.25.ends_at, ...), custom_call_target="tpu_custom_call" | custom-call | tf_op jit(solution)/shard_map/gram/pallas_call | solution.py:226
  20.4 14.4 %all_to_all.10 = f32[16,1,256]{2,1,0:T(1,128)S(1)} all-to-all(f32[16,1,256]{2,1,0:T(1,128)S(1)} %broadcast_in_dim.7), channel_id=1, replica_groups=mesh['y'=8,'x'=4,'z'=8,'core'=2] {'core','y'}, dimensions={0} | all-to-all | bytes 32768 | tf_op jit(solution)/shard_map/all_to_all | solution.py:348
  34.9 19.3 %all_to_all.11.pieces = f32[32,1,256]{2,1,0:T(1,128)S(1)} all-to-all(f32[32,1,256]{2,1,0:T(1,128)S(1)} %broadcast_in_dim.16), channel_id=1, replica_groups=mesh['y'=8,'x'=4,'z'=8,'core'=2] {'z','x'}, dimensions={0} | all-to-all | bytes 65536 | tf_op jit(solution)/shard_map/all_to_all | solution.py:348
  54.2 2.5 %orthonormal.1 = (f32[16,24,8,256]{3,2,1,0:T(8,128)}, f32[16,16]{1,0:T(8,128)}) custom-call(bf16[24,256,256]{2,1,0:T(8,128)(2,1)S(1)} %get-tuple-element.30.parts, f32[32,1,256]{2,1,0:T(1,128)S(1)} %all_to_all.11.pieces), custom_call_target="tpu_custom_call" | custom-call | tf_op jit(solution)/shard_map/orthonormal/pallas_call | solution.py:322
  (3 shorter events, 0.1 us)
Async XLA Ops:
  2.7 15.8 %collective-permute-start = (bf16[384,256]{1,0:T(8,128)(2,1)S(1)}, bf16[384,256]{1,0:T(8,128)(2,1)S(1)}, u32[]{:S(2)}, u32[]{:S(2)}) collective-permute-start(bf16[384,256]{1,0:T(8,128)(2,1)S(1)} %get-tuple-element.26), channel_id=1, source_target_pairs={{16,32},{48,64},{80,96},{112,128},{144,160},{176,192},{208,224},{2... | collective-permute-start | bytes 589832 | tf_op jit(solution)/shard_map/ppermute | solution.py:343
  3.4 15.1 %collective-permute-start.1 = (bf16[384,256]{1,0:T(8,128)(2,1)S(1)}, bf16[384,256]{1,0:T(8,128)(2,1)S(1)}, u32[]{:S(2)}, u32[]{:S(2)}) collective-permute-start(bf16[384,256]{1,0:T(8,128)(2,1)S(1)} %get-tuple-element.27), channel_id=1, source_target_pairs={{0,16},{32,48},{64,80},{96,112},{128,144},{160,176},{192,208},{224... | collective-permute-start | bytes 589832 | tf_op jit(solution)/shard_map/ppermute | solution.py:343
  9.8 8.7 %collective-permute-start.2 = (bf16[32,128]{1,0:T(8,128)(2,1)S(1)}, bf16[32,128]{1,0:T(8,128)(2,1)S(1)}, u32[]{:S(2)}, u32[]{:S(2)}) collective-permute-start(bf16[32,128]{1,0:T(8,128)(2,1)S(1)} %get-tuple-element.28), channel_id=1, source_target_pairs={{1,2},{3,4},{5,6},{7,8},{9,10},{11,12},{13,14},{2,1},{4,3},{6,5},{... | collective-permute-start | bytes 24584 | tf_op jit(solution)/shard_map/ppermute | solution.py:343
  14.9 3.6 %collective-permute-start.3 = (bf16[32,128]{1,0:T(8,128)(2,1)S(1)}, bf16[32,128]{1,0:T(8,128)(2,1)S(1)}, u32[]{:S(2)}, u32[]{:S(2)}) collective-permute-start(bf16[32,128]{1,0:T(8,128)(2,1)S(1)} %get-tuple-element.29), channel_id=1, source_target_pairs={{0,1},{2,3},{4,5},{6,7},{8,9},{10,11},{12,13},{14,15},{1,0},{3,2},... | collective-permute-start | bytes 24584 | tf_op jit(solution)/shard_map/ppermute | solution.py:343

commit v5 on v4

--- a/solution.py
+++ b/solution.py
@@ -266,9 +266,11 @@
         crosses = jnp.where(mine, cross, crosses)
         tails = jnp.where(mine, tail, tails)
         if k + 2 < PROBES:
-            over = jnp.where(row > k + 1, 1.0 / (head * tail - cross * cross), 0.0)
-            first_ratio = (tail * one - cross * two) * over
-            second_ratio = (head * two - cross * one) * over
+            inverse = 1.0 / head
+            lean = cross * inverse
+            over = jnp.where(row > k + 1, 1.0 / (tail - lean * cross), 0.0)
+            second_ratio = (two - lean * one) * over
+            first_ratio = jnp.where(row > k + 1, one * inverse, 0.0) - lean * second_ratio
             for j in range(k + 2, PROBES):
                 columns[j] = (
                     columns[j]

time: 57 us -> 57 us (level)
  no operation moved by 1% of the time
where the time goes in v5:
time: 57 us; the launch traced here: 56.7 us
  blocking collectives  33.7 us (59%)
  starting transfers between devices  14.1 us (25%)
  Pallas kernels  8.14 us (14%)
  between operations  0.72 us (1%)
    all_to_all x2, blocking collectives, all_copies(): return lax.all_to_all(copies, axes, 0, 0)  33.7 us
    ppermute x4, starting transfers between devices, swap(): return lax.ppermute(array, axis, pairs + [(j, i) for i, j in pairs])  14.1 us
    pallas_call x1, Pallas kernels, orthonormal(): pl.pallas_call(functools.partial(basis_kernel, scale), out_shape=[jax.Sha...  2.57 us
    pallas_call x1, Pallas kernels, load(): pl.pallas_call(load_kernel, out_shape=[pltpu.VMEM((SLABS * PROBES, YS), B...  2.03 us
    pallas_call x1, Pallas kernels, gram(): pl.pallas_call(gram_kernel, out_shape=[pltpu.VMEM((SLABS, 2 * BLOCK, YS),...  1.93 us
    pallas_call x1, Pallas kernels, inner(): pl.pallas_call(inner_kernel, out_shape=pltpu.VMEM((SLABS, BLOCK, YS), F32...  1.61 us
  transfers between devices with their start and end apart: 4, of which 0 were waited for; matrix products, arithmetic and copies ran while one was open for 0% of the time, Pallas kernels for 3%

profile of v5, /device:TPU:1, one launch (start us, length us, event | category | flops | bytes accessed | tf_op | source)
XLA Modules:
  0.0 56.7 jit_solution(9675759639313195983)
XLA Ops:
  0.6 2.0 %load.1 = (bf16[384,256]{1,0:T(8,128)(2,1)S(1)}, bf16[384,256]{1,0:T(8,128)(2,1)S(1)}, bf16[32,128]{1,0:T(8,128)(2,1)S(1)}, bf16[32,128]{1,0:T(8,128)(2,1)S(1)},...) custom-call(bf16[16,24,8,256]{3,2,1,0:T(8,128)(2,1)} %bitcast.4, ...), custom_call_target="tpu_custom_call" | custom-call | tf_op jit(solution)/shard_map/load/pallas_call | solution.py:111
  2.7 0.7 %collective-permute-start = (bf16[384,256]{1,0:T(8,128)(2,1)S(1)}, bf16[384,256]{1,0:T(8,128)(2,1)S(1)}, u32[]{:S(2)}, u32[]{:S(2)}) collective-permute-start(bf16[384,256]{1,0:T(8,128)(2,1)S(1)} %get-tuple-element.26), channel_id=1, source_target_pairs={{16,32},{48,64},{80,96},{112,128},{144,160},{176,192},{208,224},{2... | collective-permute-start | bytes 589832 | tf_op jit(solution)/shard_map/ppermute | solution.py:345
  3.4 6.4 %collective-permute-start.1 = (bf16[384,256]{1,0:T(8,128)(2,1)S(1)}, bf16[384,256]{1,0:T(8,128)(2,1)S(1)}, u32[]{:S(2)}, u32[]{:S(2)}) collective-permute-start(bf16[384,256]{1,0:T(8,128)(2,1)S(1)} %get-tuple-element.27), channel_id=1, source_target_pairs={{0,16},{32,48},{64,80},{96,112},{128,144},{160,176},{192,208},{224... | collective-permute-start | bytes 589832 | tf_op jit(solution)/shard_map/ppermute | solution.py:345
  9.8 5.1 %collective-permute-start.2 = (bf16[32,128]{1,0:T(8,128)(2,1)S(1)}, bf16[32,128]{1,0:T(8,128)(2,1)S(1)}, u32[]{:S(2)}, u32[]{:S(2)}) collective-permute-start(bf16[32,128]{1,0:T(8,128)(2,1)S(1)} %get-tuple-element.28), channel_id=1, source_target_pairs={{1,2},{3,4},{5,6},{7,8},{9,10},{11,12},{13,14},{2,1},{4,3},{6,5},{... | collective-permute-start | bytes 24584 | tf_op jit(solution)/shard_map/ppermute | solution.py:345
  14.9 1.9 %collective-permute-start.3 = (bf16[32,128]{1,0:T(8,128)(2,1)S(1)}, bf16[32,128]{1,0:T(8,128)(2,1)S(1)}, u32[]{:S(2)}, u32[]{:S(2)}) collective-permute-start(bf16[32,128]{1,0:T(8,128)(2,1)S(1)} %get-tuple-element.29), channel_id=1, source_target_pairs={{0,1},{2,3},{4,5},{6,7},{8,9},{10,11},{12,13},{14,15},{1,0},{3,2},... | collective-permute-start | bytes 24584 | tf_op jit(solution)/shard_map/ppermute | solution.py:345
  16.8 1.6 %inner.1.image = f32[24,128,256]{2,1,0:T(8,128)S(1)} custom-call(f32[2,24,128,128]{3,2,1,0:T(8,128)S(1)} %get-tuple-element.18.wide, f32[12,8,256]{2,1,0:T(8,128)S(1)} %get-tuple-element.19.flow, f32[12,8,256]{2,1,0:T(8,128)S(1)} %get-tuple-element.20.visc, f32[12,8,256]{2,1,0:T(8,128)S(1)} %get-tuple-element.21.brink, ...), custom_call_target="tpu_custom_call" | custom-call | flops 800000000 | bytes 6000000 | tf_op jit(solution)/shard_map/inner/pallas_call | solution.py:165
  18.4 0.0 collective-permute-done.2.y_second
  18.4 0.0 collective-permute-done.3.y_first
  18.4 0.0 collective-permute-done.x_second
  18.5 0.0 collective-permute-done.1.x_first
  18.5 1.9 %gram.1 = (bf16[24,256,256]{2,1,0:T(8,128)(2,1)S(1)}, f32[1,256]{1,0:T(1,128)S(1)}) custom-call(f32[24,128,256]{2,1,0:T(8,128)S(1)} %inner.1.image, f32[12,8,256]{2,1,0:T(8,128)S(1)} %get-tuple-element.20.visc, f32[12,8,256]{2,1,0:T(8,128)S(1)} %get-tuple-element.22.cond, bf16[24,64,256]{2,1,0:T(8,128)(2,1)S(1)} %get-tuple-element.25.ends_at, ...), custom_call_target="tpu_custom_call" | custom-call | tf_op jit(solution)/shard_map/gram/pallas_call | solution.py:226
  20.4 14.4 %all_to_all.10 = f32[16,1,256]{2,1,0:T(1,128)S(1)} all-to-all(f32[16,1,256]{2,1,0:T(1,128)S(1)} %broadcast_in_dim.7), channel_id=1, replica_groups=mesh['y'=8,'x'=4,'z'=8,'core'=2] {'core','y'}, dimensions={0} | all-to-all | bytes 32768 | tf_op jit(solution)/shard_map/all_to_all | solution.py:350
  34.9 19.3 %all_to_all.11.pieces = f32[32,1,256]{2,1,0:T(1,128)S(1)} all-to-all(f32[32,1,256]{2,1,0:T(1,128)S(1)} %broadcast_in_dim.16), channel_id=1, replica_groups=mesh['y'=8,'x'=4,'z'=8,'core'=2] {'z','x'}, dimensions={0} | all-to-all | bytes 65536 | tf_op jit(solution)/shard_map/all_to_all | solution.py:350
  54.2 2.6 %orthonormal.1 = (f32[16,24,8,256]{3,2,1,0:T(8,128)}, f32[16,16]{1,0:T(8,128)}) custom-call(bf16[24,256,256]{2,1,0:T(8,128)(2,1)S(1)} %get-tuple-element.30.parts, f32[32,1,256]{2,1,0:T(1,128)S(1)} %all_to_all.11.pieces), custom_call_target="tpu_custom_call" | custom-call | tf_op jit(solution)/shard_map/orthonormal/pallas_call | solution.py:324
  (3 shorter events, 0.1 us)
Async XLA Ops:
  2.7 15.8 %collective-permute-start = (bf16[384,256]{1,0:T(8,128)(2,1)S(1)}, bf16[384,256]{1,0:T(8,128)(2,1)S(1)}, u32[]{:S(2)}, u32[]{:S(2)}) collective-permute-start(bf16[384,256]{1,0:T(8,128)(2,1)S(1)} %get-tuple-element.26), channel_id=1, source_target_pairs={{16,32},{48,64},{80,96},{112,128},{144,160},{176,192},{208,224},{2... | collective-permute-start | bytes 589832 | tf_op jit(solution)/shard_map/ppermute | solution.py:345
  3.4 15.1 %collective-permute-start.1 = (bf16[384,256]{1,0:T(8,128)(2,1)S(1)}, bf16[384,256]{1,0:T(8,128)(2,1)S(1)}, u32[]{:S(2)}, u32[]{:S(2)}) collective-permute-start(bf16[384,256]{1,0:T(8,128)(2,1)S(1)} %get-tuple-element.27), channel_id=1, source_target_pairs={{0,16},{32,48},{64,80},{96,112},{128,144},{160,176},{192,208},{224... | collective-permute-start | bytes 589832 | tf_op jit(solution)/shard_map/ppermute | solution.py:345
  9.8 8.7 %collective-permute-start.2 = (bf16[32,128]{1,0:T(8,128)(2,1)S(1)}, bf16[32,128]{1,0:T(8,128)(2,1)S(1)}, u32[]{:S(2)}, u32[]{:S(2)}) collective-permute-start(bf16[32,128]{1,0:T(8,128)(2,1)S(1)} %get-tuple-element.28), channel_id=1, source_target_pairs={{1,2},{3,4},{5,6},{7,8},{9,10},{11,12},{13,14},{2,1},{4,3},{6,5},{... | collective-permute-start | bytes 24584 | tf_op jit(solution)/shard_map/ppermute | solution.py:345
  14.9 3.6 %collective-permute-start.3 = (bf16[32,128]{1,0:T(8,128)(2,1)S(1)}, bf16[32,128]{1,0:T(8,128)(2,1)S(1)}, u32[]{:S(2)}, u32[]{:S(2)}) collective-permute-start(bf16[32,128]{1,0:T(8,128)(2,1)S(1)} %get-tuple-element.29), channel_id=1, source_target_pairs={{0,1},{2,3},{4,5},{6,7},{8,9},{10,11},{12,13},{14,15},{1,0},{3,2},... | collective-permute-start | bytes 24584 | tf_op jit(solution)/shard_map/ppermute | solution.py:345

commit v6 on v5

--- a/solution.py
+++ b/solution.py
@@ -85,8 +85,7 @@
             for slab in range(SLABS):
                 sides = jnp.where(lane // 2 == slab, pltpu.roll(ends[slab], 2 * slab + 1, 1), sides)
             columns[rows] = sides
-    x_face(wide, XS - 1 - x_end, x_second)
-    x_face(wide, x_end, x_first)
+    x_faces(wide, x_end, x_first, x_second)
     columns[...] = columns[...].T
     high, low = columns[pl.ds(0, 32, stride=2), :], columns[pl.ds(1, 32, stride=2), :]
     y_first[...] = jnp.where(y_end == 0, low, high).astype(BF16)
@@ -97,11 +96,14 @@
         value[...] = pick(kind[...], [tables[i, j] for j in range(4)])
 
 
-def x_face(wide, end, face):
+def x_faces(wide, x_end, x_first, x_second):
     rows = wide.reshape(2, SLABS * BLOCK, 128)
     for half in range(2):
-        ends = rows[half, pl.ds(end, SLABS * PROBES, stride=XS), :]
-        face[:, half * 128 : half * 128 + 128] = ends.astype(BF16)
+        span = slice(half * 128, half * 128 + 128)
+        low = rows[half, pl.ds(0, SLABS * PROBES, stride=XS), :]
+        high = rows[half, pl.ds(XS - 1, SLABS * PROBES, stride=XS), :]
+        x_first[:, span] = jnp.where(x_end == 0, low, high).astype(BF16)
+        x_second[:, span] = jnp.where(x_end == 0, high, low).astype(BF16)
 
 
 def load(probes, material, flow, tables):

time: 57 us -> 56.9 us (level)
  no operation moved by 1% of the time
where the time goes in v6:
time: 56.9 us; the launch traced here: 56.7 us
  blocking collectives  33.7 us (59%)
  starting transfers between devices  14.1 us (25%)
  Pallas kernels  8.04 us (14%)
  between operations  0.72 us (1%)
    all_to_all x2, blocking collectives, all_copies(): return lax.all_to_all(copies, axes, 0, 0)  33.7 us
    ppermute x4, starting transfers between devices, swap(): return lax.ppermute(array, axis, pairs + [(j, i) for i, j in pairs])  14.1 us
    pallas_call x1, Pallas kernels, orthonormal(): pl.pallas_call(functools.partial(basis_kernel, scale), out_shape=[jax.Sha...  2.57 us
    pallas_call x1, Pallas kernels, load(): pl.pallas_call(load_kernel, out_shape=[pltpu.VMEM((SLABS * PROBES, YS), B...  1.94 us
    pallas_call x1, Pallas kernels, gram(): pl.pallas_call(gram_kernel, out_shape=[pltpu.VMEM((SLABS, 2 * BLOCK, YS),...  1.93 us
    pallas_call x1, Pallas kernels, inner(): pl.pallas_call(inner_kernel, out_shape=pltpu.VMEM((SLABS, BLOCK, YS), F32...  1.61 us
  transfers between devices with their start and end apart: 4, of which 0 were waited for; matrix products, arithmetic and copies ran while one was open for 0% of the time, Pallas kernels for 3%

profile of v6, /device:TPU:1, one launch (start us, length us, event | category | flops | bytes accessed | tf_op | source)
XLA Modules:
  0.0 56.7 jit_solution(8155804771641178837)
XLA Ops:
  0.6 1.9 %load.1 = (bf16[384,256]{1,0:T(8,128)(2,1)S(1)}, bf16[384,256]{1,0:T(8,128)(2,1)S(1)}, bf16[32,128]{1,0:T(8,128)(2,1)S(1)}, bf16[32,128]{1,0:T(8,128)(2,1)S(1)},...) custom-call(bf16[16,24,8,256]{3,2,1,0:T(8,128)(2,1)} %bitcast.4, ...), custom_call_target="tpu_custom_call" | custom-call | tf_op jit(solution)/shard_map/load/pallas_call | solution.py:113
  2.6 0.7 %collective-permute-start = (bf16[384,256]{1,0:T(8,128)(2,1)S(1)}, bf16[384,256]{1,0:T(8,128)(2,1)S(1)}, u32[]{:S(2)}, u32[]{:S(2)}) collective-permute-start(bf16[384,256]{1,0:T(8,128)(2,1)S(1)} %get-tuple-element.26), channel_id=1, source_target_pairs={{16,32},{48,64},{80,96},{112,128},{144,160},{176,192},{208,224},{2... | collective-permute-start | bytes 589832 | tf_op jit(solution)/shard_map/ppermute | solution.py:347
  3.3 6.4 %collective-permute-start.1 = (bf16[384,256]{1,0:T(8,128)(2,1)S(1)}, bf16[384,256]{1,0:T(8,128)(2,1)S(1)}, u32[]{:S(2)}, u32[]{:S(2)}) collective-permute-start(bf16[384,256]{1,0:T(8,128)(2,1)S(1)} %get-tuple-element.27), channel_id=1, source_target_pairs={{0,16},{32,48},{64,80},{96,112},{128,144},{160,176},{192,208},{224... | collective-permute-start | bytes 589832 | tf_op jit(solution)/shard_map/ppermute | solution.py:347
  9.7 5.1 %collective-permute-start.2 = (bf16[32,128]{1,0:T(8,128)(2,1)S(1)}, bf16[32,128]{1,0:T(8,128)(2,1)S(1)}, u32[]{:S(2)}, u32[]{:S(2)}) collective-permute-start(bf16[32,128]{1,0:T(8,128)(2,1)S(1)} %get-tuple-element.28), channel_id=1, source_target_pairs={{1,2},{3,4},{5,6},{7,8},{9,10},{11,12},{13,14},{2,1},{4,3},{6,5},{... | collective-permute-start | bytes 24584 | tf_op jit(solution)/shard_map/ppermute | solution.py:347
  14.8 1.9 %collective-permute-start.3 = (bf16[32,128]{1,0:T(8,128)(2,1)S(1)}, bf16[32,128]{1,0:T(8,128)(2,1)S(1)}, u32[]{:S(2)}, u32[]{:S(2)}) collective-permute-start(bf16[32,128]{1,0:T(8,128)(2,1)S(1)} %get-tuple-element.29), channel_id=1, source_target_pairs={{0,1},{2,3},{4,5},{6,7},{8,9},{10,11},{12,13},{14,15},{1,0},{3,2},... | collective-permute-start | bytes 24584 | tf_op jit(solution)/shard_map/ppermute | solution.py:347
  16.7 1.6 %inner.1.image = f32[24,128,256]{2,1,0:T(8,128)S(1)} custom-call(f32[2,24,128,128]{3,2,1,0:T(8,128)S(1)} %get-tuple-element.18.wide, f32[12,8,256]{2,1,0:T(8,128)S(1)} %get-tuple-element.19.flow, f32[12,8,256]{2,1,0:T(8,128)S(1)} %get-tuple-element.20.visc, f32[12,8,256]{2,1,0:T(8,128)S(1)} %get-tuple-element.21.brink, ...), custom_call_target="tpu_custom_call" | custom-call | flops 800000000 | bytes 6000000 | tf_op jit(solution)/shard_map/inner/pallas_call | solution.py:167
  18.3 0.0 collective-permute-done.2.y_second
  18.3 0.0 collective-permute-done.3.y_first
  18.3 0.0 collective-permute-done.x_second
  18.4 0.0 collective-permute-done.1.x_first
  18.4 1.9 %gram.1 = (bf16[24,256,256]{2,1,0:T(8,128)(2,1)S(1)}, f32[1,256]{1,0:T(1,128)S(1)}) custom-call(f32[24,128,256]{2,1,0:T(8,128)S(1)} %inner.1.image, f32[12,8,256]{2,1,0:T(8,128)S(1)} %get-tuple-element.20.visc, f32[12,8,256]{2,1,0:T(8,128)S(1)} %get-tuple-element.22.cond, bf16[24,64,256]{2,1,0:T(8,128)(2,1)S(1)} %get-tuple-element.25.ends_at, ...), custom_call_target="tpu_custom_call" | custom-call | tf_op jit(solution)/shard_map/gram/pallas_call | solution.py:228
  20.3 14.4 %all_to_all.10 = f32[16,1,256]{2,1,0:T(1,128)S(1)} all-to-all(f32[16,1,256]{2,1,0:T(1,128)S(1)} %broadcast_in_dim.7), channel_id=1, replica_groups=mesh['y'=8,'x'=4,'z'=8,'core'=2] {'core','y'}, dimensions={0} | all-to-all | bytes 32768 | tf_op jit(solution)/shard_map/all_to_all | solution.py:352
  34.8 19.3 %all_to_all.11.pieces = f32[32,1,256]{2,1,0:T(1,128)S(1)} all-to-all(f32[32,1,256]{2,1,0:T(1,128)S(1)} %broadcast_in_dim.16), channel_id=1, replica_groups=mesh['y'=8,'x'=4,'z'=8,'core'=2] {'z','x'}, dimensions={0} | all-to-all | bytes 65536 | tf_op jit(solution)/shard_map/all_to_all | solution.py:352
  54.1 2.6 %orthonormal.1 = (f32[16,24,8,256]{3,2,1,0:T(8,128)}, f32[16,16]{1,0:T(8,128)}) custom-call(bf16[24,256,256]{2,1,0:T(8,128)(2,1)S(1)} %get-tuple-element.30.parts, f32[32,1,256]{2,1,0:T(1,128)S(1)} %all_to_all.11.pieces), custom_call_target="tpu_custom_call" | custom-call | tf_op jit(solution)/shard_map/orthonormal/pallas_call | solution.py:326
  (3 shorter events, 0.1 us)
Async XLA Ops:
  2.6 15.8 %collective-permute-start = (bf16[384,256]{1,0:T(8,128)(2,1)S(1)}, bf16[384,256]{1,0:T(8,128)(2,1)S(1)}, u32[]{:S(2)}, u32[]{:S(2)}) collective-permute-start(bf16[384,256]{1,0:T(8,128)(2,1)S(1)} %get-tuple-element.26), channel_id=1, source_target_pairs={{16,32},{48,64},{80,96},{112,128},{144,160},{176,192},{208,224},{2... | collective-permute-start | bytes 589832 | tf_op jit(solution)/shard_map/ppermute | solution.py:347
  3.3 15.1 %collective-permute-start.1 = (bf16[384,256]{1,0:T(8,128)(2,1)S(1)}, bf16[384,256]{1,0:T(8,128)(2,1)S(1)}, u32[]{:S(2)}, u32[]{:S(2)}) collective-permute-start(bf16[384,256]{1,0:T(8,128)(2,1)S(1)} %get-tuple-element.27), channel_id=1, source_target_pairs={{0,16},{32,48},{64,80},{96,112},{128,144},{160,176},{192,208},{224... | collective-permute-start | bytes 589832 | tf_op jit(solution)/shard_map/ppermute | solution.py:347
  9.7 8.7 %collective-permute-start.2 = (bf16[32,128]{1,0:T(8,128)(2,1)S(1)}, bf16[32,128]{1,0:T(8,128)(2,1)S(1)}, u32[]{:S(2)}, u32[]{:S(2)}) collective-permute-start(bf16[32,128]{1,0:T(8,128)(2,1)S(1)} %get-tuple-element.28), channel_id=1, source_target_pairs={{1,2},{3,4},{5,6},{7,8},{9,10},{11,12},{13,14},{2,1},{4,3},{6,5},{... | collective-permute-start | bytes 24584 | tf_op jit(solution)/shard_map/ppermute | solution.py:347
  14.8 3.6 %collective-permute-start.3 = (bf16[32,128]{1,0:T(8,128)(2,1)S(1)}, bf16[32,128]{1,0:T(8,128)(2,1)S(1)}, u32[]{:S(2)}, u32[]{:S(2)}) collective-permute-start(bf16[32,128]{1,0:T(8,128)(2,1)S(1)} %get-tuple-element.29), channel_id=1, source_target_pairs={{0,1},{2,3},{4,5},{6,7},{8,9},{10,11},{12,13},{14,15},{1,0},{3,2},... | collective-permute-start | bytes 24584 | tf_op jit(solution)/shard_map/ppermute | solution.py:347

commit v7 on v6

--- a/solution.py
+++ b/solution.py
@@ -365,8 +365,8 @@
     halos = (x_second, x_first, y_second, y_first)
     image = inner(wide, flow, visc, brink, cond, along_y, along_x)
     parts, local = gram(image, visc, cond, ends_at, halos)
-    slab_sum = jnp.sum(all_copies(local, ("core", "y")), axis=0)
-    pieces = all_copies(slab_sum, ("z", "x"))
+    slab_sum = jnp.sum(all_copies(local, ("core", "z")), axis=0)
+    pieces = all_copies(slab_sum, ("y", "x"))
     rows_total = SLABS * XS * YS * lax.axis_size(GX) * lax.axis_size(GY)
     basis, factor = orthonormal(parts, pieces, math.sqrt(rows_total))
     return (basis.reshape(shape), factor)

time: 56.9 us -> 56.9 us (level)
  no operation moved by 1% of the time
where the time goes in v7:
time: 56.9 us; the launch traced here: 56.7 us
  blocking collectives  33.7 us (59%)
  starting transfers between devices  14.1 us (25%)
  Pallas kernels  8.04 us (14%)
  between operations  0.72 us (1%)
    all_to_all x2, blocking collectives, all_copies(): return lax.all_to_all(copies, axes, 0, 0)  33.7 us
    ppermute x4, starting transfers between devices, swap(): return lax.ppermute(array, axis, pairs + [(j, i) for i, j in pairs])  14.1 us
    pallas_call x1, Pallas kernels, orthonormal(): pl.pallas_call(functools.partial(basis_kernel, scale), out_shape=[jax.Sha...  2.57 us
    pallas_call x1, Pallas kernels, load(): pl.pallas_call(load_kernel, out_shape=[pltpu.VMEM((SLABS * PROBES, YS), B...  1.94 us
    pallas_call x1, Pallas kernels, gram(): pl.pallas_call(gram_kernel, out_shape=[pltpu.VMEM((SLABS, 2 * BLOCK, YS),...  1.93 us
    pallas_call x1, Pallas kernels, inner(): pl.pallas_call(inner_kernel, out_shape=pltpu.VMEM((SLABS, BLOCK, YS), F32...  1.61 us
  transfers between devices with their start and end apart: 4, of which 0 were waited for; matrix products, arithmetic and copies ran while one was open for 0% of the time, Pallas kernels for 3%

profile of v7, /device:TPU:1, one launch (start us, length us, event | category | flops | bytes accessed | tf_op | source)
XLA Modules:
  0.0 56.7 jit_solution(6998129850541098642)
XLA Ops:
  0.6 1.9 %load.1 = (bf16[384,256]{1,0:T(8,128)(2,1)S(1)}, bf16[384,256]{1,0:T(8,128)(2,1)S(1)}, bf16[32,128]{1,0:T(8,128)(2,1)S(1)}, bf16[32,128]{1,0:T(8,128)(2,1)S(1)},...) custom-call(bf16[16,24,8,256]{3,2,1,0:T(8,128)(2,1)} %bitcast.4, ...), custom_call_target="tpu_custom_call" | custom-call | tf_op jit(solution)/shard_map/load/pallas_call | solution.py:113
  2.6 0.7 %collective-permute-start = (bf16[384,256]{1,0:T(8,128)(2,1)S(1)}, bf16[384,256]{1,0:T(8,128)(2,1)S(1)}, u32[]{:S(2)}, u32[]{:S(2)}) collective-permute-start(bf16[384,256]{1,0:T(8,128)(2,1)S(1)} %get-tuple-element.26), channel_id=1, source_target_pairs={{16,32},{48,64},{80,96},{112,128},{144,160},{176,192},{208,224},{2... | collective-permute-start | bytes 589832 | tf_op jit(solution)/shard_map/ppermute | solution.py:347
  3.3 6.4 %collective-permute-start.1 = (bf16[384,256]{1,0:T(8,128)(2,1)S(1)}, bf16[384,256]{1,0:T(8,128)(2,1)S(1)}, u32[]{:S(2)}, u32[]{:S(2)}) collective-permute-start(bf16[384,256]{1,0:T(8,128)(2,1)S(1)} %get-tuple-element.27), channel_id=1, source_target_pairs={{0,16},{32,48},{64,80},{96,112},{128,144},{160,176},{192,208},{224... | collective-permute-start | bytes 589832 | tf_op jit(solution)/shard_map/ppermute | solution.py:347
  9.7 5.1 %collective-permute-start.2 = (bf16[32,128]{1,0:T(8,128)(2,1)S(1)}, bf16[32,128]{1,0:T(8,128)(2,1)S(1)}, u32[]{:S(2)}, u32[]{:S(2)}) collective-permute-start(bf16[32,128]{1,0:T(8,128)(2,1)S(1)} %get-tuple-element.28), channel_id=1, source_target_pairs={{1,2},{3,4},{5,6},{7,8},{9,10},{11,12},{13,14},{2,1},{4,3},{6,5},{... | collective-permute-start | bytes 24584 | tf_op jit(solution)/shard_map/ppermute | solution.py:347
  14.8 1.9 %collective-permute-start.3 = (bf16[32,128]{1,0:T(8,128)(2,1)S(1)}, bf16[32,128]{1,0:T(8,128)(2,1)S(1)}, u32[]{:S(2)}, u32[]{:S(2)}) collective-permute-start(bf16[32,128]{1,0:T(8,128)(2,1)S(1)} %get-tuple-element.29), channel_id=1, source_target_pairs={{0,1},{2,3},{4,5},{6,7},{8,9},{10,11},{12,13},{14,15},{1,0},{3,2},... | collective-permute-start | bytes 24584 | tf_op jit(solution)/shard_map/ppermute | solution.py:347
  16.7 1.6 %inner.1.image = f32[24,128,256]{2,1,0:T(8,128)S(1)} custom-call(f32[2,24,128,128]{3,2,1,0:T(8,128)S(1)} %get-tuple-element.18.wide, f32[12,8,256]{2,1,0:T(8,128)S(1)} %get-tuple-element.19.flow, f32[12,8,256]{2,1,0:T(8,128)S(1)} %get-tuple-element.20.visc, f32[12,8,256]{2,1,0:T(8,128)S(1)} %get-tuple-element.21.brink, ...), custom_call_target="tpu_custom_call" | custom-call | flops 800000000 | bytes 6000000 | tf_op jit(solution)/shard_map/inner/pallas_call | solution.py:167
  18.3 0.0 collective-permute-done.2.y_second
  18.3 0.0 collective-permute-done.3.y_first
  18.3 0.0 collective-permute-done.x_second
  18.4 0.0 collective-permute-done.1.x_first
  18.4 1.9 %gram.1 = (bf16[24,256,256]{2,1,0:T(8,128)(2,1)S(1)}, f32[1,256]{1,0:T(1,128)S(1)}) custom-call(f32[24,128,256]{2,1,0:T(8,128)S(1)} %inner.1.image, f32[12,8,256]{2,1,0:T(8,128)S(1)} %get-tuple-element.20.visc, f32[12,8,256]{2,1,0:T(8,128)S(1)} %get-tuple-element.22.cond, bf16[24,64,256]{2,1,0:T(8,128)(2,1)S(1)} %get-tuple-element.25.ends_at, ...), custom_call_target="tpu_custom_call" | custom-call | tf_op jit(solution)/shard_map/gram/pallas_call | solution.py:228
  20.3 16.7 %all_to_all.10 = f32[16,1,256]{2,1,0:T(1,128)S(1)} all-to-all(f32[16,1,256]{2,1,0:T(1,128)S(1)} %broadcast_in_dim.7), channel_id=1, replica_groups=mesh['y'=8,'x'=4,'z'=8,'core'=2] {'core','z'}, dimensions={0} | all-to-all | bytes 32768 | tf_op jit(solution)/shard_map/all_to_all | solution.py:352
  37.1 17.0 %all_to_all.11.pieces = f32[32,1,256]{2,1,0:T(1,128)S(1)} all-to-all(f32[32,1,256]{2,1,0:T(1,128)S(1)} %broadcast_in_dim.16), channel_id=1, replica_groups=mesh['y'=8,'x'=4,'z'=8,'core'=2] {'y','x'}, dimensions={0} | all-to-all | bytes 65536 | tf_op jit(solution)/shard_map/all_to_all | solution.py:352
  54.1 2.6 %orthonormal.1 = (f32[16,24,8,256]{3,2,1,0:T(8,128)}, f32[16,16]{1,0:T(8,128)}) custom-call(bf16[24,256,256]{2,1,0:T(8,128)(2,1)S(1)} %get-tuple-element.30.parts, f32[32,1,256]{2,1,0:T(1,128)S(1)} %all_to_all.11.pieces), custom_call_target="tpu_custom_call" | custom-call | tf_op jit(solution)/shard_map/orthonormal/pallas_call | solution.py:326
  (3 shorter events, 0.1 us)
Async XLA Ops:
  2.6 15.8 %collective-permute-start = (bf16[384,256]{1,0:T(8,128)(2,1)S(1)}, bf16[384,256]{1,0:T(8,128)(2,1)S(1)}, u32[]{:S(2)}, u32[]{:S(2)}) collective-permute-start(bf16[384,256]{1,0:T(8,128)(2,1)S(1)} %get-tuple-element.26), channel_id=1, source_target_pairs={{16,32},{48,64},{80,96},{112,128},{144,160},{176,192},{208,224},{2... | collective-permute-start | bytes 589832 | tf_op jit(solution)/shard_map/ppermute | solution.py:347
  3.3 15.1 %collective-permute-start.1 = (bf16[384,256]{1,0:T(8,128)(2,1)S(1)}, bf16[384,256]{1,0:T(8,128)(2,1)S(1)}, u32[]{:S(2)}, u32[]{:S(2)}) collective-permute-start(bf16[384,256]{1,0:T(8,128)(2,1)S(1)} %get-tuple-element.27), channel_id=1, source_target_pairs={{0,16},{32,48},{64,80},{96,112},{128,144},{160,176},{192,208},{224... | collective-permute-start | bytes 589832 | tf_op jit(solution)/shard_map/ppermute | solution.py:347
  9.7 8.7 %collective-permute-start.2 = (bf16[32,128]{1,0:T(8,128)(2,1)S(1)}, bf16[32,128]{1,0:T(8,128)(2,1)S(1)}, u32[]{:S(2)}, u32[]{:S(2)}) collective-permute-start(bf16[32,128]{1,0:T(8,128)(2,1)S(1)} %get-tuple-element.28), channel_id=1, source_target_pairs={{1,2},{3,4},{5,6},{7,8},{9,10},{11,12},{13,14},{2,1},{4,3},{6,5},{... | collective-permute-start | bytes 24584 | tf_op jit(solution)/shard_map/ppermute | solution.py:347
  14.8 3.6 %collective-permute-start.3 = (bf16[32,128]{1,0:T(8,128)(2,1)S(1)}, bf16[32,128]{1,0:T(8,128)(2,1)S(1)}, u32[]{:S(2)}, u32[]{:S(2)}) collective-permute-start(bf16[32,128]{1,0:T(8,128)(2,1)S(1)} %get-tuple-element.29), channel_id=1, source_target_pairs={{0,1},{2,3},{4,5},{6,7},{8,9},{10,11},{12,13},{14,15},{1,0},{3,2},... | collective-permute-start | bytes 24584 | tf_op jit(solution)/shard_map/ppermute | solution.py:347
